TPU v7x, 32 devices: a whole 2x2x4 slice. The times are simulated.
32 devices in a mesh: dp: 4 (over y, x), mp: 8 (over z, core).
Axes of the slice: x: 2, y: 2, z: 4, core: 2. Of those that a mesh axis runs over, the one named last changes fastest.
Arguments:
- tokens: bfloat16 [32768, 1024], P(('dp', 'mp')), may hold values from -6 to 6
- cotangent: bfloat16 [32768, 1024], P(('dp', 'mp')), may hold values from -6 to 6
- first_norm_gain: float32 [1024], replicated, may hold values from 0.25 to 1.75
- query_key_value_weight: bfloat16 [1024, 16, 192], P(None, 'mp'), may hold values from -0.1875 to 0.1875
- output_matrix: bfloat16 [16, 64, 1024], P('mp'), may hold values from -1.5 to 1.5
- second_norm_gain: float32 [1024], replicated, may hold values from 0.25 to 1.75
- up_matrix: bfloat16 [4096, 1024], P('mp'), may hold values from -0.1875 to 0.1875
- down_matrix: bfloat16 [4096, 1024], P('mp'), may hold values from -0.09375 to 0.09375
- query_down_factor: float32 [1024, 4], replicated, may hold values from -0.1875 to 0.1875
- query_adapter_up: float32 [4, 1024], replicated, may hold values from -0.3 to 0.3
- value_down_factor: float32 [1024, 4], replicated, may hold values from -0.1875 to 0.1875
- value_adapter_up: float32 [4, 1024], replicated, may hold values from -0.3 to 0.3
- counts: int32 [4, 4], P('dp'), may hold values from 2 to 8, as said below
- lengths: int32 [4, 20], P('dp'), may hold values from 65 to 1024, as said below
Outputs:
- output: bfloat16 [32768, 1024], P(('dp', 'mp'))
- input_grad: bfloat16 [32768, 1024], P(('dp', 'mp'))
- grad_a_q: float32 [1024, 4], replicated
- grad_b_q: float32 [4, 1024], replicated
- grad_a_v: float32 [1024, 4], replicated
- grad_b_v: float32 [4, 1024], replicated
Inputs may be any that keep to these rules, and one draw needn't show every extreme that they name: `counts`: each bucket's count lies between half its slots, rounded up, and all of them (4 slots, 8 for bucket 3); in every bucket some group has all its slots live. `lengths`: an item's length is more than half of its bucket's slot length and at most all of it; slot 0 is full in every group. Lengths of slots beyond a bucket's count are present but unused.
All inputs are finite; a program needn't handle non-finite values.
Results may differ from a plain program's by a relative error of at most 0.02.
Values may be sent and summed in bfloat16 or wider, within the bound.
No kernel may reach another device: no remote copies, remote signals or barrier semaphores. Data moves between devices by JAX's collectives and lax.ppermute only.
A program may use at most 256 MiB of HBM per device.

v0:
```python
import math

import jax
import jax.numpy as jnp
from jax import lax
from jax.sharding import PartitionSpec as P

BASE_LEN = 128
ITEMS = 4


norm_eps = 1e-05
adapter_scale = 8.0
top_precision = lax.Precision.HIGHEST
masked_score = -1e30


def bucket_table():
    return [
        (8 * BASE_LEN, ITEMS, 0),
        (4 * BASE_LEN, ITEMS, ITEMS),
        (2 * BASE_LEN, ITEMS, 2 * ITEMS),
        (BASE_LEN, 2 * ITEMS, 3 * ITEMS),
    ]


def token_valid(counts, lengths):
    pieces = []
    for bucket, (length, number, offset) in enumerate(bucket_table()):
        slot_ids = jnp.arange(number, dtype=jnp.int32)
        living = slot_ids < counts[bucket]
        places = jnp.arange(length, dtype=jnp.int32)
        inside = places[None, :] < lengths[offset : offset + number][:, None]
        pieces.append(jnp.logical_and(living[:, None], inside).reshape(-1))
    return jnp.concatenate(pieces).astype(jnp.float32)


def layer_norm(values, norm_gain):
    center = values - jnp.mean(values, axis=-1, keepdims=True)
    spread = jnp.mean(center * center, axis=-1, keepdims=True)
    return center * lax.rsqrt(spread + norm_eps) * norm_gain


def gelu_tanh(values):
    return jax.nn.gelu(values, approximate=True)


def contract_last(left, right):
    return lax.dot_general(
        left, right, (((1,), (1,)), ((), ())), preferred_element_type=jnp.float32
    )


def take_region(array, row_start, length, number):
    region = lax.slice_in_dim(array, row_start, row_start + length * number)
    return region.reshape((number, length) + array.shape[1:])


def allowed_pairs(valid_rows, length):
    places = jnp.arange(length, dtype=jnp.int32)
    causal = places[:, None] >= places[None, :]
    diagonal = places[:, None] == places[None, :]
    return jnp.logical_and(
        causal[None], jnp.logical_or(valid_rows[:, None, :] > 0.0, diagonal[None])
    )


def masked_scores(query_blk, key_blk, allowed, scale):
    scores = (
        jnp.einsum("nqhd,nkhd->nhqk", query_blk, key_blk, preferred_element_type=jnp.float32)
        * scale
    )
    return jnp.where(allowed[:, None], scores, masked_score)


def region_forward(query_blk, key_blk, value_blk, allowed, scale):
    scores = masked_scores(query_blk, key_blk, allowed, scale)
    row_max = jnp.max(scores, axis=-1, keepdims=True)
    raised = jnp.exp(scores - row_max)
    running = jnp.sum(raised, axis=-1, keepdims=True)
    probs_low = (raised / running).astype(jnp.bfloat16)
    attended = jnp.einsum(
        "nhqk,nkhd->nqhd", probs_low, value_blk, preferred_element_type=jnp.float32
    )
    return (attended, row_max + jnp.log(running))


def region_backward(query_blk, key_blk, value_blk, grad_blk, log_total, allowed, scale):
    scores = masked_scores(query_blk, key_blk, allowed, scale)
    probs = jnp.exp(scores - log_total)
    probs_low = probs.astype(jnp.bfloat16)
    grad_probs = jnp.einsum(
        "nqhd,nkhd->nhqk", grad_blk, value_blk, preferred_element_type=jnp.float32
    )
    inner = jnp.sum(grad_probs * probs, axis=-1, keepdims=True)
    grad_scores = (probs * (grad_probs - inner)).astype(jnp.bfloat16)
    grad_query = (
        jnp.einsum("nhqk,nkhd->nqhd", grad_scores, key_blk, preferred_element_type=jnp.float32)
        * scale
    )
    grad_key = (
        jnp.einsum("nhqk,nqhd->nkhd", grad_scores, query_blk, preferred_element_type=jnp.float32)
        * scale
    )
    grad_value = jnp.einsum(
        "nhqk,nqhd->nkhd", probs_low, grad_blk, preferred_element_type=jnp.float32
    )
    return (grad_query, grad_key, grad_value)


def shards(
    tokens,
    cotangent,
    first_norm_gain,
    query_key_value_weight,
    output_matrix,
    second_norm_gain,
    up_matrix,
    down_matrix,
    query_down_factor,
    query_adapter_up,
    value_down_factor,
    value_adapter_up,
    counts,
    lengths,
):
    local_rows = tokens.shape[0]
    model_width = tokens.shape[1]
    model_index = lax.axis_index("mp")
    heads_here = query_key_value_weight.shape[1]
    head_size = query_key_value_weight.shape[2] // 3
    head_columns = heads_here * head_size
    adapter_inner_rank = query_down_factor.shape[1]
    scale = 1.0 / math.sqrt(head_size)
    valid_all = token_valid(counts[0], lengths[0])
    rows_of_group = valid_all.shape[0]
    valid_here = lax.dynamic_slice_in_dim(valid_all, model_index * local_rows, local_rows)[:, None]
    adapter_down = jnp.concatenate([query_down_factor, value_down_factor], axis=1)
    inputs = tokens.astype(jnp.float32)
    first_normed = layer_norm(inputs, first_norm_gain).astype(jnp.bfloat16)
    rows_one_all = lax.all_gather(first_normed, "mp", axis=0, tiled=True)
    flat_qkv = query_key_value_weight.reshape(model_width, heads_here * 3 * head_size)
    projected_rows = jnp.dot(rows_one_all, flat_qkv, preferred_element_type=jnp.float32).reshape(
        rows_of_group, heads_here, 3, head_size
    )
    lowrank = jnp.dot(
        rows_one_all, adapter_down, precision=top_precision, preferred_element_type=jnp.float32
    )
    column_begin = model_index * head_columns
    query_up_factor = lax.dynamic_slice_in_dim(query_adapter_up, column_begin, head_columns, 1)
    value_up_factor = lax.dynamic_slice_in_dim(value_adapter_up, column_begin, head_columns, 1)
    query_vectors = projected_rows[:, :, 0] + adapter_scale * jnp.dot(
        lowrank[:, :adapter_inner_rank], query_up_factor, precision=top_precision
    ).reshape(rows_of_group, heads_here, head_size)
    rows_of_values = projected_rows[:, :, 2] + adapter_scale * jnp.dot(
        lowrank[:, adapter_inner_rank:], value_up_factor, precision=top_precision
    ).reshape(rows_of_group, heads_here, head_size)
    query_low = query_vectors.astype(jnp.bfloat16)
    key_low = projected_rows[:, :, 1].astype(jnp.bfloat16)
    value_low = rows_of_values.astype(jnp.bfloat16)
    attended_parts = []
    log_totals = []
    row_start = 0
    for length, number, offset in bucket_table():
        allowed = allowed_pairs(take_region(valid_all, row_start, length, number), length)
        attended, log_total = region_forward(
            take_region(query_low, row_start, length, number),
            take_region(key_low, row_start, length, number),
            take_region(value_low, row_start, length, number),
            allowed,
            scale,
        )
        attended_parts.append(attended.reshape(length * number, head_columns))
        log_totals.append(log_total)
        row_start = row_start + length * number
    attended_low = jnp.concatenate(attended_parts, axis=0).astype(jnp.bfloat16)
    out_flat = output_matrix.reshape(head_columns, model_width)
    attn_sum = lax.psum_scatter(
        jnp.dot(attended_low, out_flat, preferred_element_type=jnp.float32).astype(jnp.bfloat16),
        "mp",
        scatter_dimension=0,
        tiled=True,
    ).astype(jnp.float32)
    mid = inputs + attn_sum
    normed_two = layer_norm(mid, second_norm_gain).astype(jnp.bfloat16)
    grad_out = cotangent.astype(jnp.float32) * valid_here
    grad_out_low = grad_out.astype(jnp.bfloat16)
    rows_two_all = lax.all_gather(normed_two, "mp", axis=0, tiled=True)
    hidden_pre = contract_last(rows_two_all, up_matrix)
    hidden_low = gelu_tanh(hidden_pre).astype(jnp.bfloat16)
    mlp_sum = lax.psum_scatter(
        jnp.dot(hidden_low, down_matrix, preferred_element_type=jnp.float32).astype(jnp.bfloat16),
        "mp",
        scatter_dimension=0,
        tiled=True,
    ).astype(jnp.float32)
    grad_rows_two_all = lax.all_gather(grad_out_low, "mp", axis=0, tiled=True)
    grad_hidden = contract_last(grad_rows_two_all, down_matrix)
    gelu_unused, gelu_back = jax.vjp(gelu_tanh, hidden_pre)
    grad_pre_low = gelu_back(grad_hidden)[0].astype(jnp.bfloat16)
    grad_normed_two = lax.psum_scatter(
        jnp.dot(grad_pre_low, up_matrix, preferred_element_type=jnp.float32).astype(jnp.bfloat16),
        "mp",
        scatter_dimension=0,
        tiled=True,
    ).astype(jnp.float32)
    output = ((mid + mlp_sum) * valid_here).astype(jnp.bfloat16)
    norm_unused, norm_two_back = jax.vjp(lambda values: layer_norm(values, second_norm_gain), mid)
    grad_mid = grad_out + norm_two_back(grad_normed_two)[0]
    grad_mid_low = grad_mid.astype(jnp.bfloat16)
    grad_rows_one_all = lax.all_gather(grad_mid_low, "mp", axis=0, tiled=True)
    grad_attended = (
        contract_last(grad_rows_one_all, out_flat)
        .astype(jnp.bfloat16)
        .reshape(rows_of_group, heads_here, head_size)
    )
    grad_query_parts = []
    grad_key_parts = []
    grad_value_parts = []
    row_start = 0
    for (length, number, offset), log_total in zip(bucket_table(), log_totals):
        allowed = allowed_pairs(take_region(valid_all, row_start, length, number), length)
        grad_query, grad_key, grad_value = region_backward(
            take_region(query_low, row_start, length, number),
            take_region(key_low, row_start, length, number),
            take_region(value_low, row_start, length, number),
            take_region(grad_attended, row_start, length, number),
            log_total,
            allowed,
            scale,
        )
        grad_query_parts.append(grad_query.reshape(length * number, heads_here, head_size))
        grad_key_parts.append(grad_key.reshape(length * number, heads_here, head_size))
        grad_value_parts.append(grad_value.reshape(length * number, heads_here, head_size))
        row_start = row_start + length * number
    grad_query_low = jnp.concatenate(grad_query_parts, axis=0).astype(jnp.bfloat16)
    grad_key_low = jnp.concatenate(grad_key_parts, axis=0).astype(jnp.bfloat16)
    grad_value_low = jnp.concatenate(grad_value_parts, axis=0).astype(jnp.bfloat16)
    grad_query_flat = grad_query_low.reshape(rows_of_group, head_columns)
    grad_value_flat = grad_value_low.reshape(rows_of_group, head_columns)
    query_reduced_gradient = adapter_scale * jnp.dot(
        grad_query_flat,
        query_up_factor.T,
        precision=top_precision,
        preferred_element_type=jnp.float32,
    )
    value_reduced_gradient = adapter_scale * jnp.dot(
        grad_value_flat,
        value_up_factor.T,
        precision=top_precision,
        preferred_element_type=jnp.float32,
    )
    grad_lowrank = jnp.concatenate([query_reduced_gradient, value_reduced_gradient], axis=1)
    grad_qkv_low = jnp.stack([grad_query_low, grad_key_low, grad_value_low], axis=2).reshape(
        rows_of_group, heads_here * 3 * head_size
    )
    partial_rows = contract_last(grad_qkv_low, flat_qkv)
    grad_normed_one = lax.psum_scatter(
        (
            partial_rows
            + jnp.dot(
                grad_lowrank,
                adapter_down.T,
                precision=top_precision,
                preferred_element_type=jnp.float32,
            )
        ).astype(jnp.bfloat16),
        "mp",
        scatter_dimension=0,
        tiled=True,
    ).astype(jnp.float32)
    grad_a_part = lax.dot_general(
        rows_one_all,
        grad_lowrank,
        (((0,), (0,)), ((), ())),
        precision=top_precision,
        preferred_element_type=jnp.float32,
    )
    query_up_gradient_share = adapter_scale * lax.dot_general(
        lowrank[:, :adapter_inner_rank],
        grad_query_flat,
        (((0,), (0,)), ((), ())),
        precision=top_precision,
        preferred_element_type=jnp.float32,
    )
    value_up_gradient_share = adapter_scale * lax.dot_general(
        lowrank[:, adapter_inner_rank:],
        grad_value_flat,
        (((0,), (0,)), ((), ())),
        precision=top_precision,
        preferred_element_type=jnp.float32,
    )
    zero_cols = jnp.zeros((adapter_inner_rank, model_width), jnp.float32)
    grad_bq_full = lax.dynamic_update_slice_in_dim(
        zero_cols, query_up_gradient_share, column_begin, 1
    )
    grad_bv_full = lax.dynamic_update_slice_in_dim(
        zero_cols, value_up_gradient_share, column_begin, 1
    )
    grad_a_all, grad_bq_all, grad_bv_all = lax.psum(
        (grad_a_part, grad_bq_full, grad_bv_full), ("dp", "mp")
    )
    norm_unused, norm_one_back = jax.vjp(lambda values: layer_norm(values, first_norm_gain), inputs)
    input_grad = (grad_mid + norm_one_back(grad_normed_one)[0]).astype(jnp.bfloat16)
    return (
        output,
        input_grad,
        grad_a_all[:, :adapter_inner_rank],
        grad_bq_all,
        grad_a_all[:, adapter_inner_rank:],
        grad_bv_all,
    )


def solution(mesh):
    in_specs = (
        P(("dp", "mp"), None),
        P(("dp", "mp"), None),
        P(),
        P(None, "mp", None),
        P("mp", None, None),
        P(),
        P("mp", None),
        P("mp", None),
        P(),
        P(),
        P(),
        P(),
        P("dp", None),
        P("dp", None),
    )
    out_specs = (P(("dp", "mp"), None), P(("dp", "mp"), None), P(), P(), P(), P())
    return jax.shard_map(shards, mesh=mesh, in_specs=in_specs, out_specs=out_specs, check_vma=False)
```

profile of v0, /device:TPU:0, one launch (start us, length us, event | category | flops | bytes accessed | tf_op | source)
XLA Modules:
  0.0 1831.2 jit_solution(1312558356280242697)
XLA Ops:
  7.3 2.1 convert_reduce_fusion
  9.4 2.3 fusion.26
  12.9 2.0 fusion.28
  22.4 4.1 or_and_fusion
  26.5 142.4 %all-gather.5.cloned.1.call-done = bf16[8192,1024]{1,0:T(8,128)(2,1)} async-done(((bf16[1024,1024]{1,0:T(8,128)(2,1)}), bf16[8192,1024]{1,0:T(8,128)(2,1)}) %all-gather.5.cloned.1.call-update) | async-done | bytes 16777232 | tf_op jit(solution)/shard_map/all_gather | solution.py:141
  168.9 20.0 %fusion.190 = (bf16[8192,2,3,64]{0,3,2,1:T(8,128)(2,1)S(1)}, f32[8192,2,3,64]{0,3,2,1:T(8,128)}) fusion(bf16[2,3,64,1024]{3,2,1,0:T(8,128)(2,1)} %bitcast.356, bf16[8192,1024]{1,0:T(8,128)(2,1)} %all-gather.5.cloned.1.call-done), kind=kOutput, calls=%fused_computation.301 | convolution fusion | flops 6445596672 | bytes 36438016 | tf_op jit(solution)/shard_map/dot_general | solution.py:143
  191.6 16.8 fusion.145
  208.4 4.2 convolution_multiply_fusion
  212.6 5.7 convolution_multiply_fusion.1
  218.3 7.1 fusion.35
  225.4 1.9 slice.195
  227.3 2.3 slice.190
  230.4 2.0 fusion.186
  233.5 2.3 reshape.652
  235.8 2.7 reshape.648
  238.5 1.9 reshape.656
  246.7 2.5 fusion.193
  250.5 2.1 copy-done.4
  255.4 16.9 fusion.194
  272.3 13.2 fusion
  285.5 13.9 fusion.62
  301.6 11.9 convolution_convert_fusion
  313.5 166.6 %reduce-scatter.5.cloned.1.call-done = bf16[1024,1024]{1,0:T(8,128)(2,1)} async-done(((bf16[8192,1024]{1,0:T(8,128)(2,1)}), bf16[1024,1024]{1,0:T(8,128)(2,1)}) %reduce-scatter.5.cloned.1.call-update) | async-done | bytes 2097168 | tf_op jit(solution)/shard_map/reduce_scatter | solution.py:178
  480.1 2.4 fusion.40
  483.4 2.2 multiply_convert_fusion.5
  485.7 3.3 fusion.37
  489.1 146.2 %all-gather.7.cloned.1.call-done = bf16[8192,1024]{1,0:T(8,128)(2,1)} async-done(((bf16[1024,1024]{1,0:T(8,128)(2,1)}), bf16[8192,1024]{1,0:T(8,128)(2,1)}) %all-gather.7.cloned.1.call-update) | async-done | bytes 16777232 | tf_op jit(solution)/shard_map/all_gather | solution.py:188
  635.3 16.3 fusion.197
  651.6 135.1 %all-gather.9.cloned.1.call-done = bf16[8192,1024]{1,0:T(8,128)(2,1)} async-done(((bf16[1024,1024]{1,0:T(8,128)(2,1)}), bf16[8192,1024]{1,0:T(8,128)(2,1)}) %all-gather.9.cloned.1.call-update) | async-done | bytes 16777232 | tf_op jit(solution)/shard_map/all_gather | solution.py:197
  786.7 32.2 %convolution_convert_fusion.1 = bf16[8192,1024]{1,0:T(8,128)(2,1)} fusion(bf16[512,1024]{1,0:T(8,128)(2,1)} %param.20, f32[8192,512]{1,0:T(8,128)} %fusion.197, bf16[8192,1024]{1,0:T(8,128)(2,1)} %all-gather.9.cloned.1.call-done, bf16[512,1024]{1,0:T(8,128)(2,1)S(1)} %copy-done), kind=kOutput, calls=%fused_computation.26 | convolution fusion | flops 17272143872 | bytes 52428800 | tf_op jit(solution)/shard_map/dot_general | solution.py:202
  819.0 17.8 convolution_convert_fusion.2
  836.9 148.7 %reduce-scatter.9.cloned.1.call-done = bf16[1024,1024]{1,0:T(8,128)(2,1)} async-done(((bf16[8192,1024]{1,0:T(8,128)(2,1)}), bf16[1024,1024]{1,0:T(8,128)(2,1)}) %reduce-scatter.9.cloned.1.call-update) | async-done | bytes 2097168 | tf_op jit(solution)/shard_map/reduce_scatter | solution.py:201
  985.5 3.5 multiply_reduce_fusion.2
  989.0 165.4 %reduce-scatter.7.cloned.1.call-done = bf16[1024,1024]{1,0:T(8,128)(2,1)} async-done(((bf16[8192,1024]{1,0:T(8,128)(2,1)}), bf16[1024,1024]{1,0:T(8,128)(2,1)}) %reduce-scatter.7.cloned.1.call-update) | async-done | bytes 2097168 | tf_op jit(solution)/shard_map/reduce_scatter | solution.py:191
  1154.4 5.4 fusion.182
  1159.8 2.0 copy-done.6
  1161.9 2.0 fusion.42
  1164.1 149.4 %all-gather.11.cloned.1.call-done = bf16[8192,1024]{1,0:T(8,128)(2,1)} async-done(((bf16[1024,1024]{1,0:T(8,128)(2,1)}), bf16[8192,1024]{1,0:T(8,128)(2,1)}) %all-gather.11.cloned.1.call-update) | async-done | bytes 16777232 | tf_op jit(solution)/shard_map/all_gather | solution.py:211
  1313.5 8.5 convolution_convert_fusion.3
  1336.3 2.4 reshape.670
  1339.5 5.7 fusion.71
  1345.3 4.6 multiply_reduce_fusion.1
  1349.9 2.6 multiply_convert_fusion.3
  1352.6 2.2 fusion.69
  1358.7 13.5 fusion.56
  1372.2 21.6 %multiply_reduce_fusion = (f32[4,2,1024]{2,1,0:T(2,128)S(1)}, f32[4,2,1024,1024]{2,3,1,0:T(8,128)}) fusion(f32[4,2,1024,1024]{2,3,1,0:T(8,128)} %get-tuple-element.44, f32[4,2,1024]{2,1,0:T(2,128)S(1)} %bitcast.359, bf16[4,1024,2,64]{1,3,2,0:T(8,128)(2,1)S(1)} %copy.89, bf16[2,8,4,8,1024]{4,3,2,1,0:T(8,128)(2,1)S(1)} %bitcast.324), kind=kOutput, calls=%fused_computation.2 | convolution fusion | flops 1098899456 | bytes 69271552 | tf_op jit(solution)/shard_map/nqhd,nkhd->nhqk/dot_general | solution.py:92
  1393.9 27.9 %multiply_convert_fusion = bf16[4,2,1024,1024]{2,3,1,0:T(8,128)(2,1)} fusion(f32[4,2,1024,1024]{2,3,1,0:T(8,128)} %get-tuple-element.46, f32[4,2,1024,1024]{2,3,1,0:T(8,128)} %get-tuple-element.44, f32[4,2,1024]{2,1,0:T(2,128)S(1)} %get-tuple-element.45, f32[4,2,1024]{2,1,0:T(2,128)S(1)} %bitcast.360), kind=kLoop, calls=%fused_computation.1 | loop fusion | flops 33554432 | bytes 83951616 | tf_op jit(solution)/shard_map/convert_element_type | solution.py:96
  1421.9 12.1 fusion.60
  1433.9 9.9 fusion.59
  1453.1 1.8 concatenate.107
  1457.5 1.7 fusion.87
  1468.4 2.0 copy.93
  1470.5 1.8 copy.114
  1472.3 2.6 concatenate.102
  1478.4 2.1 convolution_multiply_fusion.3
  1483.0 3.5 copy.136
  1486.5 30.6 %fusion.140 = f32[8192,1024]{1,0:T(8,128)} fusion(f32[8192,4]{0,1:T(4,128)S(1)} %convolution_multiply_fusion.2, f32[8192,4]{0,1:T(4,128)S(1)} %convolution_multiply_fusion.3, f32[1024,4]{0,1:T(4,128)S(1)} %copy-done.80, f32[1024,4]{0,1:T(4,128)S(1)} %copy-done.82), kind=kOutput, calls=%fused_computation.210 | convolution fusion | flops 805380096 | bytes 33849344 | tf_op jit(solution)/shard_map/dot_general | solution.py:261
  1517.2 7.2 fusion.139
  1524.5 21.0 %add_convert_fusion = bf16[8192,1024]{1,0:T(8,128)(2,1)} fusion(f32[8192,1024]{1,0:T(8,128)} %fusion.140, bf16[8192,384]{0,1:T(8,128)(2,1)} %bitcast.316, bf16[1024,384]{0,1:T(8,128)(2,1)S(1)} %bitcast.357), kind=kOutput, calls=%fused_computation | convolution fusion | flops 6459228160 | bytes 57409536 | tf_op jit(solution)/shard_map/dot_general | solution.py:49
  1545.6 96.1 %all-reduce.3.cloned.1.call-done = (f32[1024,8]{0,1:T(8,128)}, f32[4,1024]{1,0:T(4,128)}, f32[4,1024]{1,0:T(4,128)}) async-done(((f32[1024,8]{0,1:T(8,128)}, f32[4,1024]{1,0:T(4,128)}, f32[4,1024]{1,0:T(4,128)}), (f32[1024,8]{0,1:T(8,128)}, f32[4,1024]{1,0:T(4,128)}, f32[4,1024]{1,0:T(4,128)})) %all-reduce.3.cloned.1.call-update) | async-done | bytes 65552 | tf_op jit(solution)/shard_map/psum | solution.py:300
  1643.1 170.4 %reduce-scatter.11.cloned.1.call-done = bf16[1024,1024]{1,0:T(8,128)(2,1)} async-done(((bf16[8192,1024]{1,0:T(8,128)(2,1)}), bf16[1024,1024]{1,0:T(8,128)(2,1)}) %reduce-scatter.11.cloned.1.call-update) | async-done | bytes 2097168 | tf_op jit(solution)/shard_map/reduce_scatter | solution.py:258
  1813.6 2.7 fusion.29
  1816.4 3.4 fusion.41
  1819.8 3.3 add_convert_fusion.1
  (356 shorter events, 75.4 us)
Async XLA Ops:
  7.2 779.5 %copy-start = (bf16[512,1024]{1,0:T(8,128)(2,1)S(1)}, bf16[512,1024]{1,0:T(8,128)(2,1)}, u32[]{:S(2)}) copy-start(bf16[512,1024]{1,0:T(8,128)(2,1)} %param.21) | copy-start | bytes 3145732
  7.2 5.7 copy-start.2
  7.2 5.7 copy-start.69
  7.2 161.7 %all-gather.5.cloned.1.call-start = ((), (), s32[]{:S(2)}) async-start(), calls=%async_computation.4 | async-start | bytes 18874368 | tf_op jit(solution)/shard_map/all_gather | solution.py:141
  9.4 5.6 copy-start.98
  9.4 6.8 copy-start.99
  14.9 465.2 %reduce-scatter.5.cloned.1.call-start = ((), (), s32[]{:S(2)}) async-start(), calls=%async_computation.5 | async-start | bytes 18874368 | tf_op jit(solution)/shard_map/reduce_scatter | solution.py:178
  18.7 1141.1 %copy-start.67 = (f32[1024]{0:T(1024)}, f32[1024]{0:T(1024)S(1)}, u32[]{:S(2)}) copy-start(f32[1024]{0:T(1024)S(1)} %get-tuple-element.26) | copy-start | bytes 12292
  208.4 9.9 copy-start.15
  272.3 13.2 copy-start.17
  313.5 169.9 %copy-start.87 = (f32[1024]{0:T(1024)S(1)}, f32[1024]{0:T(1024)}, u32[]{:S(2)}) copy-start(f32[1024]{0:T(1024)} %param.19) | copy-start | bytes 12292
  313.5 321.8 %all-gather.7.cloned.1.call-start = ((), (), s32[]{:S(2)}) async-start(), calls=%async_computation.6 | async-start | bytes 18874368 | tf_op jit(solution)/shard_map/all_gather | solution.py:188
  485.6 301.0 %all-gather.9.cloned.1.call-start = ((), (), s32[]{:S(2)}) async-start(), calls=%async_computation.8 | async-start | bytes 18874368 | tf_op jit(solution)/shard_map/all_gather | solution.py:197
  489.0 496.5 %reduce-scatter.9.cloned.1.call-start = ((), (), s32[]{:S(2)}) async-start(), calls=%async_computation.9 | async-start | bytes 18874368 | tf_op jit(solution)/shard_map/reduce_scatter | solution.py:201
  818.9 335.5 %reduce-scatter.7.cloned.1.call-start = ((), (), s32[]{:S(2)}) async-start(), calls=%async_computation.7 | async-start | bytes 18874368 | tf_op jit(solution)/shard_map/reduce_scatter | solution.py:191
  836.8 476.7 %all-gather.11.cloned.1.call-start = ((), (), s32[]{:S(2)}) async-start(), calls=%async_computation.10 | async-start | bytes 18874368 | tf_op jit(solution)/shard_map/all_gather | solution.py:211
  1154.4 7.4 copy-start.10
  1159.8 4.1 copy-start.83
  1161.9 151.6 %copy-start.63 = (bf16[2,64,1024]{2,1,0:T(8,128)(2,1)S(1)}, bf16[2,64,1024]{2,1,0:T(8,128)(2,1)}, u32[]{:S(2)}) copy-start(bf16[2,64,1024]{2,1,0:T(8,128)(2,1)} %param.18) | copy-start | bytes 786436
  1163.9 477.8 %all-reduce.3.cloned.1.call-start = ((), (), s32[]{:S(2)}) async-start(), calls=%async_computation.12 | async-start | bytes 131072 | tf_op jit(solution)/shard_map/psum | solution.py:300
  1325.9 4.1 copy-start.52
  1327.1 5.4 copy-start.9
  1328.9 4.2 copy-start.58
  1339.5 5.8 copy-start.28
  1339.5 10.3 slice-start
  1345.3 4.6 slice-start.1
  1358.7 13.5 copy-start.18
  1393.9 28.0 %copy-start.20 = (bf16[4096,2,64]{0,2,1:T(8,128)(2,1)S(1)}, bf16[4096,2,64]{0,2,1:T(8,128)(2,1)}, u32[]{:S(2)}) copy-start(bf16[4096,2,64]{0,2,1:T(8,128)(2,1)} %slice.193) | copy-start | bytes 3145732
  1421.9 12.1 copy-start.21
  1433.9 9.9 copy-start.38
  1443.9 6.4 copy-start.56
  1443.9 6.6 copy-start.55
  1455.3 4.2 copy-start.53
  1459.2 11.3 copy-start.78
  1460.6 9.9 copy-start.24
  1476.8 5.4 copy-start.22
  1476.8 5.4 copy-start.25
  1476.9 5.4 copy-start.26
  1476.9 5.4 copy-start.35
  1476.9 5.4 copy-start.36
  1476.9 5.4 copy-start.37
  1476.9 5.4 copy-start.40
  1476.9 5.4 copy-start.41
  1476.9 5.4 copy-start.42
  1476.9 5.4 copy-start.43
  1476.9 5.4 copy-start.44
  1477.0 5.4 copy-start.45
  1483.0 34.2 %slice-start.2 = ((s8[16777216]{0:T(1024)(128)(4,1)}), s8[4194304]{0:T(1024)(128)(4,1)S(1)}, s32[]{:S(2)}) async-start(s8[16777216]{0:T(1024)(128)(4,1)} %bitcast.314), calls=%async_computation.15 | async-start | bytes 8388608
  1486.5 30.7 %slice-start.3 = ((s8[16777216]{0:T(1024)(128)(4,1)}), s8[4194304]{0:T(1024)(128)(4,1)S(1)}, s32[]{:S(2)}) async-start(s8[16777216]{0:T(1024)(128)(4,1)} %bitcast.314), calls=%async_computation.16 | async-start | bytes 8388608
  1486.5 30.7 %slice-start.4 = ((s8[16777216]{0:T(1024)(128)(4,1)}), s8[4194304]{0:T(1024)(128)(4,1)S(1)}, s32[]{:S(2)}) async-start(s8[16777216]{0:T(1024)(128)(4,1)} %bitcast.314), calls=%async_computation.17 | async-start | bytes 8388608
  1486.5 30.7 %slice-start.5 = ((s8[16777216]{0:T(1024)(128)(4,1)}), s8[4194304]{0:T(1024)(128)(4,1)S(1)}, s32[]{:S(2)}) async-start(s8[16777216]{0:T(1024)(128)(4,1)} %bitcast.314), calls=%async_computation.18 | async-start | bytes 8388608
  1517.2 7.3 copy-start.62
  1524.5 289.1 %reduce-scatter.11.cloned.1.call-start = ((), (), s32[]{:S(2)}) async-start(), calls=%async_computation.11 | async-start | bytes 18874368 | tf_op jit(solution)/shard_map/reduce_scatter | solution.py:258
  1545.6 268.0 %copy-start.3 = (bf16[1024,1024]{1,0:T(8,128)(2,1)S(1)}, bf16[1024,1024]{1,0:T(8,128)(2,1)}, u32[]{:S(2)}) copy-start(bf16[1024,1024]{1,0:T(8,128)(2,1)} %param.14) | copy-start | bytes 6291460
  1545.6 268.0 %copy-start.66 = (f32[1024]{0:T(1024)S(1)}, f32[1024]{0:T(1024)}, u32[]{:S(2)}) copy-start(f32[1024]{0:T(1024)} %copy-done.65) | copy-start | bytes 12292
  1545.6 268.0 %copy-start.70 = (f32[1024]{0:T(1024)S(1)}, f32[1024]{0:T(1024)}, u32[]{:S(2)}) copy-start(f32[1024]{0:T(1024)} %param.16) | copy-start | bytes 12292
  1545.6 270.7 %copy-start.86 = (f32[1024]{0:T(1024)S(1)}, f32[1024]{0:T(1024)}, u32[]{:S(2)}) copy-start(f32[1024]{0:T(1024)} %copy-done.85) | copy-start | bytes 12292
  1545.6 270.7 %copy-start.72 = (f32[1024]{0:T(1024)S(1)}, f32[1024]{0:T(1024)}, u32[]{:S(2)}) copy-start(f32[1024]{0:T(1024)} %copy-done.71) | copy-start | bytes 12292
  1643.1 176.6 %copy-start.68 = (f32[1024]{0:T(1024)S(1)}, f32[1024]{0:T(1024)}, u32[]{:S(2)}) copy-start(f32[1024]{0:T(1024)} %copy-done.67) | copy-start | bytes 12292
  1643.1 176.6 %copy-start.84 = (f32[1024]{0:T(1024)S(1)}, f32[1024]{0:T(1024)}, u32[]{:S(2)}) copy-start(f32[1024]{0:T(1024)} %copy-done.83) | copy-start | bytes 12292
  1813.6 6.2 copy-start.7
  1813.6 6.2 copy-start.11
  1813.6 6.2 copy-start.12
  1819.7 4.6 copy-start.1
  (52 other events, 128.9 us)
Sparse Core Ops, SparseCore 0:
  15.0 153.8 all-gather.4
  313.6 166.4 reduce-scatter.4
  485.8 149.4 all-gather.6
  637.3 149.3 all-gather.8
  819.0 166.4 reduce-scatter.8
  987.8 166.5 reduce-scatter.6
  1164.0 149.4 all-gather.10
  1524.6 117.0 all-reduce.2
  1644.1 169.4 reduce-scatter.10
where the time goes:
time: 1840 us; the launch traced here: 1830 us
  waiting for transfers between devices  1320 us (72%)
  matrix products  317 us (17%)
  other arithmetic  99.9 us (5%)
  local copies, waits for them, and re-layouts  77.3 us (4%)
    reduce_scatter x1, waiting for transfers between devices, shards(): lax.psum_scatter((partial_rows + jnp.dot(grad_lowrank, adapter_down.T, pr...  170 us
    reduce_scatter x1, waiting for transfers between devices, shards(): lax.psum_scatter(jnp.dot(attended_low, out_flat, preferred_element_type=j...  167 us
    reduce_scatter x1, waiting for transfers between devices, shards(): lax.psum_scatter(jnp.dot(hidden_low, down_matrix, preferred_element_type=...  165 us
    all_gather x1, waiting for transfers between devices, shards(): grad_rows_one_all = lax.all_gather(grad_mid_low, 'mp', axis=0, tiled=True)  149 us
    reduce_scatter x1, waiting for transfers between devices, shards(): lax.psum_scatter(jnp.dot(grad_pre_low, up_matrix, preferred_element_type=...  149 us
    all_gather x1, waiting for transfers between devices, shards(): rows_two_all = lax.all_gather(normed_two, 'mp', axis=0, tiled=True)  146 us
    all_gather x1, waiting for transfers between devices, shards(): rows_one_all = lax.all_gather(first_normed, 'mp', axis=0, tiled=True)  142 us
    all_gather x1, waiting for transfers between devices, shards(): grad_rows_two_all = lax.all_gather(grad_out_low, 'mp', axis=0, tiled=True)  135 us
  transfers between devices with their start and end apart: 9, of which 9 were waited for; matrix products, arithmetic and copies ran while one was open for 4% of the time, Pallas kernels for 0%

commit v1 on v0

--- a/solution.py
+++ b/solution.py
@@ -1,18 +1,340 @@
+import functools
 import math
 
 import jax
 import jax.numpy as jnp
+import numpy as np
 from jax import lax
+from jax.experimental import pallas as pl
+from jax.experimental.pallas import tpu as pltpu
 from jax.sharding import PartitionSpec as P
 
 BASE_LEN = 128
 ITEMS = 4
-
+BLOCK = 256
+VMEM_LIMIT = 56 * 1024 * 1024
 
 norm_eps = 1e-05
 adapter_scale = 8.0
 top_precision = lax.Precision.HIGHEST
 masked_score = -1e30
+f32 = jnp.float32
+bf16 = jnp.bfloat16
+
+
+def dot_nn(a, b):
+    return lax.dot_general(a, b, (((1,), (0,)), ((), ())), preferred_element_type=f32)
+
+
+def dot_nt(a, b):
+    return lax.dot_general(a, b, (((1,), (1,)), ((), ())), preferred_element_type=f32)
+
+
+def dot_tn(a, b):
+    return lax.dot_general(a, b, (((0,), (0,)), ((), ())), preferred_element_type=f32)
+
+
+def split_hi_lo(v):
+    hi = v.astype(bf16)
+    return hi, (v - hi.astype(f32)).astype(bf16)
+
+
+def whole(a):
+    return pl.BlockSpec(a.shape, lambda *i: (0,) * a.ndim)
+
+
+def params():
+    return pltpu.CompilerParams(vmem_limit_bytes=VMEM_LIMIT)
+
+
+def attn_fwd_kernel(n_ref, w_ref, e_ref, lr_ref, kaug_ref, qaug_ref, bias_ref, qkv_ref, o_ref, lse_ref):
+    rows = n_ref.shape[0]
+    w = w_ref[0].reshape(384, w_ref.shape[3])
+    res = dot_nt(w, n_ref[...]) + dot_nn(e_ref[0], lr_ref[...])
+    low = res.astype(bf16)
+    for h in range(2):
+        a, b = h * 192, h * 192 + 96
+        q = jnp.concatenate([low[a : a + 32], low[b : b + 32]], axis=0) * bf16(0.125)
+        k = jnp.concatenate([low[a + 32 : a + 64], low[b + 32 : b + 64]], axis=0)
+        v = jnp.concatenate([low[a + 64 : a + 96], low[b + 64 : b + 96]], axis=0)
+        qkv_ref[0, h * 192 : h * 192 + 64] = q
+        qkv_ref[0, h * 192 + 64 : h * 192 + 128] = k
+        qkv_ref[0, h * 192 + 128 : h * 192 + 192] = v
+        qa = jnp.concatenate([q, qaug_ref[...]], axis=0)
+        ka = jnp.concatenate([k, kaug_ref[...]], axis=0)
+        for ib in range(rows // BLOCK):
+            here = slice(ib * BLOCK, (ib + 1) * BLOCK)
+            upto = (ib + 1) * BLOCK
+            s = dot_tn(ka[:, :upto], qa[:, here])
+            diag = s[ib * BLOCK :] + bias_ref[ib]
+            s = jnp.concatenate([s[: ib * BLOCK], diag], axis=0) if ib else diag
+            top = jnp.max(s, axis=0, keepdims=True)
+            p = jnp.exp(s - top)
+            total = jnp.sum(p, axis=0, keepdims=True)
+            o = dot_nn(v[:, :upto], p.astype(bf16)) * (1.0 / total)
+            o_ref[0, h * 64 : (h + 1) * 64, here] = o.astype(bf16)
+            lse_ref[0, h : h + 1, here] = top + jnp.log(total)
+
+
+def attn_fwd(normed, w, e, lr, kaug, qaug, bias):
+    shards = w.shape[0]
+    rows, width = normed.shape
+    return pl.pallas_call(
+        attn_fwd_kernel,
+        grid=(shards,),
+        in_specs=[
+            whole(normed),
+            pl.BlockSpec((1, 4, 96, width), lambda i: (i, 0, 0, 0)),
+            pl.BlockSpec((1,) + e.shape[1:], lambda i: (i, 0, 0)),
+            whole(lr), whole(kaug), whole(qaug), whole(bias),
+        ],
+        out_specs=[
+            pl.BlockSpec((1, 384, rows), lambda i: (i, 0, 0)),
+            pl.BlockSpec((1, 128, rows), lambda i: (i, 0, 0)),
+            pl.BlockSpec((1, 2, rows), lambda i: (i, 0, 0)),
+        ],
+        out_shape=[
+            jax.ShapeDtypeStruct((shards, 384, rows), bf16),
+            jax.ShapeDtypeStruct((shards, 128, rows), bf16),
+            jax.ShapeDtypeStruct((shards, 2, rows), f32),
+        ],
+        compiler_params=params(),
+    )(normed, w, e, lr, kaug, qaug, bias)
+
+
+def norm_stats(v):
+    center = v - jnp.mean(v, axis=-1, keepdims=True)
+    r = lax.rsqrt(jnp.mean(center * center, axis=-1, keepdims=True) + norm_eps)
+    return center * r, r
+
+
+def norm_back(n, r, f):
+    return r * (f - jnp.mean(f, axis=-1, keepdims=True) - n * jnp.mean(f * n, axis=-1, keepdims=True))
+
+
+def out_proj_kernel(o_ref, w_ref, x_ref, gain_ref, mid_ref, n_ref):
+    width = x_ref.shape[1]
+    o = o_ref[...].reshape(width, BLOCK)
+    w = w_ref[...].reshape(width, width)
+    mid = x_ref[...].astype(f32) + dot_tn(o, w)
+    n, r = norm_stats(mid)
+    mid_ref[...] = mid
+    n_ref[...] = (n * gain_ref[...]).astype(bf16)
+
+
+def out_proj(o, w, x, gain):
+    rows, width = x.shape
+    shards = o.shape[0]
+    blk = pl.BlockSpec((BLOCK, width), lambda i: (i, 0))
+    return pl.pallas_call(
+        out_proj_kernel,
+        grid=(rows // BLOCK,),
+        in_specs=[
+            pl.BlockSpec((shards, 128, BLOCK), lambda i: (0, 0, i)),
+            pl.BlockSpec((shards, 4, 32, width), lambda i: (0, 0, 3, 0)),
+            blk,
+            whole(gain),
+        ],
+        out_specs=[blk, blk],
+        out_shape=[jax.ShapeDtypeStruct((rows, width), f32), jax.ShapeDtypeStruct((rows, width), bf16)],
+        compiler_params=params(),
+    )(o, w, x, gain)
+
+
+GELU_C = math.sqrt(2.0 / math.pi)
+
+
+def mlp_kernel(n_ref, g_ref, b_ref, mid_ref, valid_ref, gain_ref, wo_ref, out_ref, gmid_ref, do_ref, mlp_acc, gnt_acc, *, chunk):
+    step = pl.program_id(0)
+    rows, width = n_ref.shape
+
+    @pl.when(step == 0)
+    def _():
+        mlp_acc[...] = jnp.zeros_like(mlp_acc)
+        gnt_acc[...] = jnp.zeros_like(gnt_acc)
+
+    up = b_ref[0, :, :128].reshape(512, width)
+    down = b_ref[0, :, 128:].reshape(512, width)
+
+    @pl.loop(0, rows // chunk)
+    def _(c):
+        at = pl.ds(pl.multiple_of(c * chunk, chunk), chunk)
+        u = dot_nt(n_ref[at, :], up)
+        gh = dot_nt(g_ref[at, :], down)
+        uu = u * u
+        th = jnp.tanh(u * (GELU_C + (GELU_C * 0.044715) * uu))
+        half = 0.5 + 0.5 * th
+        hidden = u * half
+        slope = half + (0.5 * u) * (1.0 - th * th) * (GELU_C + (3.0 * 0.044715 * GELU_C) * uu)
+        mlp_acc[at, :] += dot_nn(hidden.astype(bf16), down)
+        gnt_acc[at, :] += dot_nn((gh * slope).astype(bf16), up)
+
+    @pl.when(step == pl.num_programs(0) - 1)
+    def _():
+        wo = wo_ref[...].reshape(width, width)
+
+        @pl.loop(0, rows // BLOCK)
+        def _(c):
+            at = pl.ds(pl.multiple_of(c * BLOCK, BLOCK), BLOCK)
+            mid = mid_ref[at, :]
+            out_ref[at, :] = ((mid + mlp_acc[at, :]) * valid_ref[at, :]).astype(bf16)
+            n, r = norm_stats(mid)
+            gmid = g_ref[at, :].astype(f32) + norm_back(n, r, gnt_acc[at, :] * gain_ref[...])
+            gmid_ref[at, :] = gmid
+            do_ref[:, :, at] = dot_nt(wo, gmid.astype(bf16)).astype(bf16).reshape(do_ref.shape[0], 128, BLOCK)
+
+
+def mlp(normed, g, b, mid, valid, gain, a, chunk=512):
+    rows, width = normed.shape
+    shards = b.shape[0]
+    return pl.pallas_call(
+        functools.partial(mlp_kernel, chunk=chunk),
+        grid=(shards,),
+        in_specs=[
+            whole(normed), whole(g),
+            pl.BlockSpec((1,) + b.shape[1:], lambda i: (i, 0, 0, 0)),
+            whole(mid), whole(valid), whole(gain),
+            pl.BlockSpec((shards, 4, 32, width), lambda i: (0, 0, 3, 0)),
+        ],
+        out_specs=[
+            pl.BlockSpec((rows, width), lambda i: (0, 0)),
+            pl.BlockSpec((rows, width), lambda i: (0, 0)),
+            pl.BlockSpec((shards, 128, rows), lambda i: (0, 0, 0)),
+        ],
+        out_shape=[
+            jax.ShapeDtypeStruct((rows, width), bf16),
+            jax.ShapeDtypeStruct((rows, width), f32),
+            jax.ShapeDtypeStruct((shards, 128, rows), bf16),
+        ],
+        scratch_shapes=[pltpu.VMEM((rows, width), f32)] * 2,
+        compiler_params=params(),
+    )(normed, g, b, mid, valid, gain, a)
+
+
+def attn_bwd_kernel(qkv_ref, o_ref, do_ref, lse_ref, kaug_ref, qaug_ref, bias_ref, et_ref, lrs_ref, dqkv_ref, gl_ref, gb_ref, dk_acc, dv_acc):
+    rows = qkv_ref.shape[2]
+    step = pl.program_id(0)
+    for h in range(2):
+        c = h * 192
+        q, k, v = (qkv_ref[0, c + 64 * t : c + 64 * t + 64] for t in range(3))
+        qa = jnp.concatenate([q, qaug_ref[...]], axis=0)
+        ka = jnp.concatenate([k, kaug_ref[...]], axis=0)
+        for ib in range(rows // BLOCK):
+            here = slice(ib * BLOCK, (ib + 1) * BLOCK)
+            upto = (ib + 1) * BLOCK
+            do = do_ref[0, h * 64 : (h + 1) * 64, here]
+            o = o_ref[0, h * 64 : (h + 1) * 64, here]
+            inner = jnp.sum(do.astype(f32) * o.astype(f32), axis=0, keepdims=True)
+            s = dot_tn(ka[:, :upto], qa[:, here])
+            diag = s[ib * BLOCK :] + bias_ref[ib]
+            s = jnp.concatenate([s[: ib * BLOCK], diag], axis=0) if ib else diag
+            p = jnp.exp(s - lse_ref[0, h : h + 1, here])
+            dp = dot_tn(v[:, :upto], do)
+            ds = (p * (dp - inner)).astype(bf16)
+            pb = p.astype(bf16)
+            dq = (dot_nn(k[:, :upto], ds) * 0.125).astype(bf16)
+            dqkv_ref[0, c : c + 32, here] = dq[:32]
+            dqkv_ref[0, c + 96 : c + 128, here] = dq[32:]
+            dk = dot_nt(q[:, here], ds)
+            dv = dot_nt(do, pb)
+            if ib:
+                dk_acc[:, : ib * BLOCK] += dk[:, : ib * BLOCK]
+                dv_acc[:, : ib * BLOCK] += dv[:, : ib * BLOCK]
+            dk_acc[:, here] = dk[:, ib * BLOCK :]
+            dv_acc[:, here] = dv[:, ib * BLOCK :]
+        for t, acc in ((32, dk_acc), (64, dv_acc)):
+            low = acc[...].astype(bf16)
+            dqkv_ref[0, c + t : c + t + 32] = low[:32]
+            dqkv_ref[0, c + 96 + t : c + 128 + t] = low[32:]
+    d = dqkv_ref[0]
+    gl = dot_nn(et_ref[0], d)
+    gl = gl[:8] + gl[8:]
+
+    @pl.when(step == 0)
+    def _():
+        gl_ref[...] = gl
+
+    @pl.when(step > 0)
+    def _():
+        gl_ref[...] += gl
+
+    gb = dot_nt(lrs_ref[...], d)
+    gb_ref[0] = gb[:8] + gb[8:]
+
+
+def attn_bwd(qkv, o, do, lse, kaug, qaug, bias, et, lrs):
+    shards, _, rows = qkv.shape
+    return pl.pallas_call(
+        attn_bwd_kernel,
+        grid=(shards,),
+        in_specs=[
+            pl.BlockSpec((1, 384, rows), lambda i: (i, 0, 0)),
+            pl.BlockSpec((1, 128, rows), lambda i: (i, 0, 0)),
+            pl.BlockSpec((1, 128, rows), lambda i: (i, 0, 0)),
+            pl.BlockSpec((1, 2, rows), lambda i: (i, 0, 0)),
+            whole(kaug), whole(qaug), whole(bias),
+            pl.BlockSpec((1, 16, 384), lambda i: (i, 0, 0)),
+            whole(lrs),
+        ],
+        out_specs=[
+            pl.BlockSpec((1, 384, rows), lambda i: (i, 0, 0)),
+            pl.BlockSpec((8, rows), lambda i: (0, 0)),
+            pl.BlockSpec((1, 8, 384), lambda i: (i, 0, 0)),
+        ],
+        out_shape=[
+            jax.ShapeDtypeStruct((shards, 384, rows), bf16),
+            jax.ShapeDtypeStruct((8, rows), f32),
+            jax.ShapeDtypeStruct((shards, 8, 384), f32),
+        ],
+        scratch_shapes=[pltpu.VMEM((64, rows), f32)] * 2,
+        compiler_params=params(),
+    )(qkv, o, do, lse, kaug, qaug, bias, et, lrs)
+
+
+def grad_a_kernel(gl_ref, n_ref, out_ref):
+    hi, lo = split_hi_lo(gl_ref[...])
+    out_ref[...] = dot_nn(hi, n_ref[...]) + dot_nn(lo, n_ref[...])
+
+
+def grad_a_rows(gl, normed):
+    return pl.pallas_call(
+        grad_a_kernel,
+        out_shape=jax.ShapeDtypeStruct((8, normed.shape[1]), f32),
+        compiler_params=params(),
+    )(gl, normed)
+
+
+def input_grad_kernel(d_ref, w_ref, gl_ref, dn_ref, x_ref, gmid_ref, gain_ref, out_ref):
+    width = x_ref.shape[1]
+    d = d_ref[...].reshape(-1, BLOCK)
+    w = w_ref[...].reshape(-1, width)
+    hi, lo = split_hi_lo(gl_ref[...])
+    dhi, dlo = split_hi_lo(dn_ref[...])
+    g = dot_tn(d, w)
+    g += dot_tn(jnp.concatenate([hi, lo, hi], axis=0), jnp.concatenate([dhi, dhi, dlo], axis=0))
+    n, r = norm_stats(x_ref[...].astype(f32))
+    out_ref[...] = (gmid_ref[...] + norm_back(n, r, g * gain_ref[...])).astype(bf16)
+
+
+def input_grad_rows(d, w, gl, down_t, x, gmid, gain):
+    rows, width = x.shape
+    shards = d.shape[0]
+    blk = pl.BlockSpec((BLOCK, width), lambda i: (i, 0))
+    return pl.pallas_call(
+        input_grad_kernel,
+        grid=(rows // BLOCK,),
+        in_specs=[
+            pl.BlockSpec((shards, 384, BLOCK), lambda i: (0, 0, i)),
+            pl.BlockSpec((shards, 4, 96, width), lambda i: (0, 0, 0, 0)),
+            pl.BlockSpec((8, BLOCK), lambda i: (0, i)),
+            whole(down_t),
+            blk, blk,
+            whole(gain),
+        ],
+        out_specs=blk,
+        out_shape=jax.ShapeDtypeStruct((rows, width), bf16),
+        compiler_params=params(),
+    )(d, w, gl, down_t, x, gmid, gain)
 
 
 def bucket_table():
@@ -35,6 +357,136 @@
     return jnp.concatenate(pieces).astype(jnp.float32)
 
 
+def slot_begins():
+    begins = []
+    at = 0
+    for length, number, _ in bucket_table():
+        for _ in range(number):
+            begins.append(np.full((length,), at, np.int32))
+            at += length
+    return np.concatenate(begins)
+
+
+def attention_masks(valid, begin):
+    rows = valid.shape[0]
+    blocks = rows // BLOCK
+    at = jnp.arange(rows, dtype=jnp.int32)
+    place = at.reshape(blocks, BLOCK)
+    key_place, query_place = place[:, :, None], place[:, None, :]
+    allowed = (
+        (key_place <= query_place)
+        & (key_place >= begin.reshape(blocks, 1, BLOCK))
+        & ((valid.reshape(blocks, BLOCK, 1) > 0.0) | (key_place == query_place))
+    )
+    bias = jnp.where(allowed, 0.0, masked_score).astype(f32)
+    block_id = jnp.arange(16, dtype=jnp.int32)[:, None]
+    first = jnp.pad(begin[::BLOCK], (0, 16 - blocks))[:, None]
+    own = at[None, :] // BLOCK == block_id
+    open_pair = own | ((at[None, :] >= first) & (valid[None, :] > 0.0))
+    kaug = jnp.where(open_pair | (block_id >= blocks), 0.0, masked_score).astype(bf16)
+    qaug = jnp.where(own, 1.0, 0.0).astype(bf16)
+    return bias, kaug, qaug
+
+
+def exact_hi_lo(v):
+    hi = lax.reduce_precision(v, 8, 7)
+    return hi.astype(bf16), (v - hi).astype(bf16)
+
+
+def xor_sum(v, axis, size):
+    step = 1
+    while step < size:
+        v = v + lax.ppermute(v, axis, [(i, i ^ step) for i in range(size)])
+        step *= 2
+    return v
+
+
+def whole_item_shards(
+    tokens,
+    cotangent,
+    first_norm_gain,
+    query_key_value_weight,
+    output_matrix,
+    second_norm_gain,
+    up_matrix,
+    down_matrix,
+    query_down_factor,
+    query_adapter_up,
+    value_down_factor,
+    value_adapter_up,
+    counts,
+    lengths,
+):
+    rows, width = tokens.shape
+    heads_here = query_key_value_weight.shape[1]
+    dp_size = lax.axis_size("dp")
+    mp_size = lax.axis_size("mp")
+    model_index = lax.axis_index("mp")
+    group_index = lax.axis_index("dp")
+    shards = mp_size
+    qkv_t = jnp.transpose(query_key_value_weight.reshape(width, 2, 3, 2, 32), (1, 3, 2, 4, 0)).reshape(4, 96, width)
+    a_own = jnp.concatenate([qkv_t, output_matrix.reshape(4, 32, width)], axis=1)
+    b_own = jnp.concatenate([up_matrix.reshape(4, 128, width), down_matrix.reshape(4, 128, width)], axis=1)
+    a_piece = lax.dynamic_slice_in_dim(a_own, group_index, 1, 0)
+    b_piece = lax.dynamic_slice_in_dim(b_own, group_index, 1, 0)
+    a_all = lax.all_gather(a_piece, ("mp", "dp"), axis=0, tiled=True).reshape(shards, 4, 128, width)
+    b_all = lax.all_gather(b_piece, ("mp", "dp"), axis=0, tiled=True).reshape(shards, 4, 256, width)
+
+    valid_all = token_valid(counts[0], lengths[0])
+    valid = lax.dynamic_slice_in_dim(valid_all, model_index * rows, rows)
+    begin = lax.dynamic_slice_in_dim(jnp.asarray(slot_begins()), model_index * rows, rows) - model_index * rows
+    bias, kaug, qaug = attention_masks(valid, begin)
+    valid_col = valid[:, None]
+
+    x = tokens.astype(f32)
+    center = x - jnp.mean(x, axis=-1, keepdims=True)
+    spread = jnp.mean(center * center, axis=-1, keepdims=True)
+    normed = (center * lax.rsqrt(spread + norm_eps) * first_norm_gain).astype(bf16)
+    grad_out_low = (cotangent.astype(f32) * valid_col).astype(bf16)
+
+    down_t = jnp.concatenate([query_down_factor, value_down_factor], axis=1).T
+    dhi, dlo = exact_hi_lo(down_t)
+    lowrank = lax.dot_general(
+        jnp.concatenate([dhi, dlo], axis=0), normed, (((1,), (1,)), ((), ())), preferred_element_type=f32
+    )
+    lowrank = lowrank[:8] + lowrank[8:]
+    lhi, llo = exact_hi_lo(lowrank)
+    lr = jnp.concatenate([lhi, llo, lhi, jnp.zeros_like(lhi)], axis=0)
+    lrs = jnp.concatenate([lhi, llo], axis=0)
+
+    qu = adapter_scale * query_adapter_up.reshape(4, shards, 4, 1, 32)
+    vu = adapter_scale * value_adapter_up.reshape(4, shards, 4, 1, 32)
+    zero = jnp.zeros_like(qu)
+    factor = jnp.concatenate(
+        [jnp.concatenate([qu, zero, zero], axis=3), jnp.concatenate([zero, zero, vu], axis=3)], axis=0
+    ).reshape(8, shards, 384)
+    fhi, flo = exact_hi_lo(factor)
+    e = jnp.transpose(jnp.concatenate([fhi, fhi, flo, jnp.zeros_like(fhi)], axis=0), (1, 2, 0))
+    et = jnp.transpose(jnp.concatenate([fhi, flo], axis=0), (1, 0, 2))
+
+    gain_one = first_norm_gain[None, :]
+    gain_two = second_norm_gain[None, :]
+    qkv, attended, lse = attn_fwd(normed, a_all, e, lr, kaug, qaug, bias)
+    mid, normed_two = out_proj(attended, a_all, tokens, gain_two)
+    output, grad_mid, grad_attended = mlp(normed_two, grad_out_low, b_all, mid, valid_col, gain_two, a_all)
+    d, gl, gb = attn_bwd(qkv, attended, grad_attended, lse, kaug, qaug, bias, et, lrs)
+    ga = grad_a_rows(gl, normed)
+    gb = gb.reshape(shards, 2, 4, 4, 3, 32)
+    gbq = jnp.transpose(gb[:, 0, :, :, 0], (1, 0, 2, 3)).reshape(4, width)
+    gbv = jnp.transpose(gb[:, 1, :, :, 2], (1, 0, 2, 3)).reshape(4, width)
+    packed = jnp.concatenate([ga, adapter_scale * gbq, adapter_scale * gbv], axis=0)
+    packed = xor_sum(xor_sum(packed, "mp", mp_size), "dp", dp_size)
+    input_grad = input_grad_rows(d, a_all, gl, down_t, tokens, grad_mid, gain_one)
+    return (
+        output,
+        input_grad,
+        packed[0:4].T,
+        packed[8:12],
+        packed[4:8].T,
+        packed[12:16],
+    )
+
+
 def layer_norm(values, norm_gain):
     center = values - jnp.mean(values, axis=-1, keepdims=True)
     spread = jnp.mean(center * center, axis=-1, keepdims=True)
@@ -108,7 +560,7 @@
     return (grad_query, grad_key, grad_value)
 
 
-def shards(
+def split_item_shards(
     tokens,
     cotangent,
     first_norm_gain,
@@ -330,4 +782,11 @@
         P("dp", None),
     )
     out_specs = (P(("dp", "mp"), None), P(("dp", "mp"), None), P(), P(), P(), P())
-    return jax.shard_map(shards, mesh=mesh, in_specs=in_specs, out_specs=out_specs, check_vma=False)
+    whole_items = slot_begins().shape[0] // mesh.shape["mp"] == 8 * BASE_LEN and mesh.shape["dp"] == 4
+    return jax.shard_map(
+        whole_item_shards if whole_items else split_item_shards,
+        mesh=mesh,
+        in_specs=in_specs,
+        out_specs=out_specs,
+        check_vma=False,
+    )

time: 1840 us -> 347 us (0.19)
  waiting for transfers between devices: 1320 us -> 142 us
  matrix products: 317 us -> 0.64 us
  Pallas kernels: 0 us -> 159 us
  other arithmetic: 99.9 us -> 17.3 us
  local copies, waits for them, and re-layouts: 77.3 us -> 8.37 us
    reduce_scatter x4 -> x0, waiting for transfers between devices: 651 us -> none  [the longest x1 170 us: shards(): lax.psum_scatter((partial_rows + jnp.dot(grad_lowrank, adapter_down.T, pr...]
    all_gather x4 -> x2, waiting for transfers between devices: 573 us -> 130 us  [the longest x1 68 us: whole_item_shards(): lax.all_gather(b_piece, ('mp', 'dp'), axis=0, tiled=True)]
    dot_general x40 -> x1, matrix products: 317 us -> 0.64 us  [whole_item_shards(): lax.dot_general(jnp.concatenate([dhi, dlo], axis=0), normed, (((1,), (1,)...]
    pallas_call x0 -> x6, Pallas kernels: none -> 159 us  [the longest x1 54.8 us: mlp(): pl.pallas_call(functools.partial(mlp_kernel, chunk=chunk), grid=(shards,)...]
    psum x1 -> x0, waiting for transfers between devices: 96.1 us -> none  [shards(): lax.psum((grad_a_part, grad_bq_full, grad_bv_full), ('dp', 'mp'))]
    convert_element_type x11 -> x6, other arithmetic: 51.2 us -> 3.16 us  [the longest x1 1.72 us: whole_item_shards(): grad_out_low = (cotangent.astype(f32) * valid_col).astype(bf16)]
    reduce_sum x12 -> x2, other arithmetic: 37.5 us -> 1.04 us  [the longest x1 0.69 us: whole_item_shards(): spread = jnp.mean(center * center, axis=-1, keepdims=True)]
  transfers between devices with their start and end apart: 9 -> 7, of which waited for: 9 -> 6; matrix products, arithmetic and copies ran while one was open for 4% -> 5% of each run, Pallas kernels for 0% -> 18%
where the time goes in v1:
time: 347 us; the launch traced here: 346 us
  Pallas kernels  159 us (46%)
  waiting for transfers between devices  142 us (41%)
  other arithmetic  17.3 us (5%)
  between operations  14.4 us (4%)
  local copies, waits for them, and re-layouts  8.37 us (2%)
  starting transfers between devices  5.27 us (2%)
    all_gather x1, waiting for transfers between devices, whole_item_shards(): lax.all_gather(b_piece, ('mp', 'dp'), axis=0, tiled=True)  68 us
    all_gather x1, waiting for transfers between devices, whole_item_shards(): lax.all_gather(a_piece, ('mp', 'dp'), axis=0, tiled=True)  61.5 us
    pallas_call x1, Pallas kernels, mlp(): pl.pallas_call(functools.partial(mlp_kernel, chunk=chunk), grid=(shards,)...  54.8 us
    pallas_call x1, Pallas kernels, attn_fwd(): pl.pallas_call(attn_fwd_kernel, grid=(shards,), in_specs=[whole(normed),...  40.9 us
    pallas_call x1, Pallas kernels, attn_bwd(): pl.pallas_call(attn_bwd_kernel, grid=(shards,), in_specs=[pl.BlockSpec((1...  38.9 us
    pallas_call x1, Pallas kernels, input_grad_rows(): pl.pallas_call(input_grad_kernel, grid=(rows // BLOCK,), in_specs=[pl.Blo...  13.7 us
    ppermute x5, waiting for transfers between devices, xor_sum(): v = v + lax.ppermute(v, axis, [(i, i ^ step) for i in range(size)])  12.1 us
    pallas_call x1, Pallas kernels, out_proj(): pl.pallas_call(out_proj_kernel, grid=(rows // BLOCK,), in_specs=[pl.Block...  7.48 us
  transfers between devices with their start and end apart: 7, of which 6 were waited for; matrix products, arithmetic and copies ran while one was open for 5% of the time, Pallas kernels for 18%

profile of v1, /device:TPU:0, one launch (start us, length us, event | category | flops | bytes accessed | tf_op | source)
XLA Modules:
  0.0 346.3 jit_solution(5610665231331588265)
XLA Ops:
  7.2 0.0 all-gather.3.cloned.1.call-start
  7.3 1.2 copy.36
  8.5 1.7 fusion.6
  10.2 0.0 all-gather.3.cloned.1.call-update
  10.3 0.0 all-gather.5.cloned.1.call-start
  10.3 1.9 fusion.5
  12.2 0.0 all-gather.5.cloned.1.call-update
  12.2 0.7 dynamic-slice_subtract_fusion
  12.9 0.1 slice.61
  13.0 0.6 fusion.35
  13.6 0.6 iota_compare_fusion.12
  14.3 0.1 slice_bitcast_fusion.5
  14.3 0.1 fusion.18
  14.4 0.7 iota_compare_fusion.11
  15.1 0.1 fusion.20
  15.2 0.7 iota_compare_fusion.10
  15.8 0.1 fusion.27
  15.9 0.7 iota_compare_fusion.9
  16.6 0.1 slice_bitcast_fusion.2
  16.6 0.1 fusion.29
  16.8 0.1 mul.90
  16.9 0.1 mul.92
  17.0 0.2 select_maximum_fusion
  17.2 0.3 reshape.237
  17.5 0.1 pad.31.clone
  17.6 0.1 maximum_bitcast_fusion
  17.7 1.2 copy.41.e_ref
  18.9 1.0 copy.42.valid_ref
  20.0 0.3 convert_reduce_fusion
  20.4 0.7 fusion.2
  21.1 0.7 fusion.4.n_ref
  21.8 1.3 copy-done.1
  23.1 0.6 fusion.13
  23.8 0.6 pad_maximum_fusion.1.lrs_ref
  24.4 0.6 maximum_bitcast_fusion.1.et_ref
  25.0 0.7 maximum_maximum_fusion.lr_ref
  25.7 0.7 select_convert_fusion
  26.4 1.3 and_select_fusion.bias_ref
  27.7 1.7 multiply_convert_fusion.g_ref
  29.5 61.5 %all-gather.3.cloned.1.call-done = bf16[32,128,1024]{2,1,0:T(8,128)(2,1)} async-done(((bf16[1,128,1024]{2,1,0:T(8,128)(2,1)}), bf16[32,128,1024]{2,1,0:T(8,128)(2,1)}) %all-gather.3.cloned.1.call-update) | async-done | bytes 8388624 | tf_op jit(solution)/shard_map/all_gather | solution.py:432
  91.0 40.9 %shard_map.190 = (bf16[8,384,1024]{2,1,0:T(8,128)(2,1)}, bf16[8,128,1024]{2,1,0:T(8,128)(2,1)}, f32[8,2,1024]{2,1,0:T(2,128)}) custom-call(bf16[1024,1024]{1,0:T(8,128)(2,1)} %copy-done.1, bf16[8,4,128,1024]{3,2,1,0:T(8,128)(2,1)} %bitcast.57, bf16[8,384,32]{2,1,0:T(8,128)(2,1)} %copy.41.e_ref, bf16[32,1024]{1,0:T(8,128)(2,1)} %maximum_maximum_fusion.lr_ref, ...), custom_call_target="tpu_custom_call" | custom-call | tf_op jit(solution)/shard_map/pallas_call | solution.py:82
  131.9 7.5 %shard_map.191 = (f32[1024,1024]{1,0:T(8,128)}, bf16[1024,1024]{1,0:T(8,128)(2,1)}) custom-call(bf16[8,128,1024]{2,1,0:T(8,128)(2,1)} %get-tuple-element.17.o_ref, bf16[8,4,128,1024]{3,2,1,0:T(8,128)(2,1)} %bitcast.58, bf16[1024,1024]{1,0:T(8,128)(2,1)} %x_ref.3, f32[1,1024]{1,0:T(1,128)} %bitcast.72), custom_call_target="tpu_custom_call" | custom-call | tf_op jit(solution)/shard_map/pallas_call | solution.py:129
  139.4 68.0 %all-gather.5.cloned.1.call-done = bf16[32,256,1024]{2,1,0:T(8,128)(2,1)} async-done(((bf16[1,256,1024]{2,1,0:T(8,128)(2,1)}), bf16[32,256,1024]{2,1,0:T(8,128)(2,1)}) %all-gather.5.cloned.1.call-update) | async-done | bytes 16777232 | tf_op jit(solution)/shard_map/all_gather | solution.py:433
  207.4 54.8 %shard_map.192 = (bf16[1024,1024]{1,0:T(8,128)(2,1)}, f32[1024,1024]{1,0:T(8,128)}, bf16[8,128,1024]{2,1,0:T(8,128)(2,1)}) custom-call(bf16[1024,1024]{1,0:T(8,128)(2,1)} %get-tuple-element.18.n_ref, bf16[1024,1024]{1,0:T(8,128)(2,1)} %multiply_convert_fusion.g_ref, bf16[8,4,256,1024]{3,2,1,0:T(8,128)(2,1)} %bitcast.61, ...), custom_call_target="tpu_custom_call" | custom-call | tf_op jit(solution)/shard_map/pallas_call | solution.py:190
  262.2 38.9 %shard_map.193 = (bf16[8,384,1024]{2,1,0:T(8,128)(2,1)}, f32[8,1024]{1,0:T(8,128)}, f32[8,8,384]{2,1,0:T(8,128)}) custom-call(bf16[8,384,1024]{2,1,0:T(8,128)(2,1)} %get-tuple-element.21.qkv_ref, bf16[8,128,1024]{2,1,0:T(8,128)(2,1)} %get-tuple-element.17.o_ref, bf16[8,128,1024]{2,1,0:T(8,128)(2,1)} %get-tuple-element.22.do_ref, ...), custom_call_target="tpu_custom_call" | custom-call | tf_op jit(solution)/shard_map/pallas_call | solution.py:267
  301.1 2.9 shard_map.195
  304.0 1.2 reshape.241
  305.2 0.1 slice_multiply_fusion.1
  305.4 0.1 mul.103
  305.5 0.1 mul.99
  305.6 0.8 pad_maximum_fusion
  306.4 0.3 collective-permute-start
  306.7 1.0 collective-permute-done
  307.7 0.8 fusion.32
  308.5 0.5 collective-permute-start.1
  308.9 3.9 %collective-permute-done.1 = f32[16,1024]{1,0:T(8,128)S(1)} collective-permute-done((f32[16,1024]{1,0:T(8,128)S(1)}, f32[16,1024]{1,0:T(8,128)S(1)}, u32[]{:S(2)}, u32[]{:S(2)}) %collective-permute-start.1) | collective-permute-done | bytes 65568 | tf_op jit(solution)/shard_map/ppermute | solution.py:399
  312.8 1.6 collective-permute-start.2
  314.4 4.2 %collective-permute-done.2 = f32[16,1024]{1,0:T(8,128)S(1)} collective-permute-done((f32[16,1024]{1,0:T(8,128)S(1)}, f32[16,1024]{1,0:T(8,128)S(1)}, u32[]{:S(2)}, u32[]{:S(2)}) %collective-permute-start.2) | collective-permute-done | bytes 65568 | tf_op jit(solution)/shard_map/ppermute | solution.py:399
  318.6 1.3 collective-permute-start.3
  319.9 3.0 collective-permute-done.3
  322.9 1.5 collective-permute-start.4
  324.5 0.6 maximum_bitcast_fusion.2.dn_ref
  325.1 13.7 %shard_map.194 = bf16[1024,1024]{1,0:T(8,128)(2,1)} custom-call(bf16[8,384,1024]{2,1,0:T(8,128)(2,1)} %get-tuple-element.24.d_ref, bf16[8,4,128,1024]{3,2,1,0:T(8,128)(2,1)} %bitcast.60, f32[8,1024]{1,0:T(8,128)} %get-tuple-element.25.gl_ref, f32[8,1024]{1,0:T(8,128)} %maximum_bitcast_fusion.2.dn_ref, bf16[1024,1024]{1,0:T(8,128)(2,1)} %x_ref.3, ...), custom_call_target="tpu_custom_call" | custom-call | tf_op jit(solution)/shard_map/pallas_call | solution.py:323
  338.8 0.6 fusion.34
  (44 shorter events, 0.3 us)
Async XLA Ops:
  7.2 5.8 %copy-start.8 = (s32[1,4]{1,0:T(1,128)S(1)}, s32[1,4]{1,0:T(1,128)}, u32[]{:S(2)}) copy-start(s32[1,4]{1,0:T(1,128)} %param.27) | copy-start | bytes 52
  7.2 7.1 %copy-start.9 = (s32[1,20]{1,0:T(1,128)S(1)}, s32[1,20]{1,0:T(1,128)}, u32[]{:S(2)}) copy-start(s32[1,20]{1,0:T(1,128)} %param.28) | copy-start | bytes 244
  7.2 9.6 %copy-start.6 = (f32[4,1024]{1,0:T(4,128)S(1)}, f32[4,1024]{1,0:T(4,128)}, u32[]{:S(2)}) copy-start(f32[4,1024]{1,0:T(4,128)} %param.24) | copy-start | bytes 49156
  7.2 9.7 %copy-start.7 = (f32[4,1024]{1,0:T(4,128)S(1)}, f32[4,1024]{1,0:T(4,128)}, u32[]{:S(2)}) copy-start(f32[4,1024]{1,0:T(4,128)} %param.26) | copy-start | bytes 49156
  7.2 83.8 %all-gather.3.cloned.1.call-start = ((), (), s32[]{:S(2)}) async-start(), calls=%async_computation | async-start | bytes 8650752 | tf_op jit(solution)/shard_map/all_gather | solution.py:432
  8.5 11.5 %copy-start.3 = (f32[1024,4]{0,1:T(4,128)S(1)}, f32[1024,4]{0,1:T(4,128)}, u32[]{:S(2)}) copy-start(f32[1024,4]{0,1:T(4,128)} %param.25) | copy-start | bytes 49156
  8.5 11.5 %copy-start.4 = (f32[1024,4]{0,1:T(4,128)S(1)}, f32[1024,4]{0,1:T(4,128)}, u32[]{:S(2)}) copy-start(f32[1024,4]{0,1:T(4,128)} %param.23) | copy-start | bytes 49156
  8.5 11.5 %copy-start = (bf16[1024,1024]{1,0:T(8,128)(2,1)S(1)}, bf16[1024,1024]{1,0:T(8,128)(2,1)}, u32[]{:S(2)}) copy-start(bf16[1024,1024]{1,0:T(8,128)(2,1)} %x_ref.3) | copy-start | bytes 6291460
  10.3 197.1 %all-gather.5.cloned.1.call-start = ((), (), s32[]{:S(2)}) async-start(), calls=%async_computation.1 | async-start | bytes 17301504 | tf_op jit(solution)/shard_map/all_gather | solution.py:433
  12.2 8.9 %copy-start.5 = (f32[1024]{0:T(1024)S(1)}, f32[1024]{0:T(1024)}, u32[]{:S(2)}) copy-start(f32[1024]{0:T(1024)} %param.17) | copy-start | bytes 12292
  21.1 6.7 %copy-start.2 = (bf16[1024,1024]{1,0:T(8,128)(2,1)S(1)}, bf16[1024,1024]{1,0:T(8,128)(2,1)}, u32[]{:S(2)}) copy-start(bf16[1024,1024]{1,0:T(8,128)(2,1)} %param.16) | copy-start | bytes 6291460
  21.8 1.3 copy-start.1
  306.4 1.3 collective-permute-start
  308.5 4.3 %collective-permute-start.1 = (f32[16,1024]{1,0:T(8,128)S(1)}, f32[16,1024]{1,0:T(8,128)S(1)}, u32[]{:S(2)}, u32[]{:S(2)}) collective-permute-start(f32[16,1024]{1,0:T(8,128)S(1)} %fusion.32), channel_id=1, source_target_pairs={{0,2},{1,3},{2,0},{3,1},{4,6},{5,7},{6,4},{7,5},{8,10},{9,11},{10,... | collective-permute-start | bytes 196616 | tf_op jit(solution)/shard_map/ppermute | solution.py:399
  312.8 5.8 %collective-permute-start.2 = (f32[16,1024]{1,0:T(8,128)S(1)}, f32[16,1024]{1,0:T(8,128)S(1)}, u32[]{:S(2)}, u32[]{:S(2)}) collective-permute-start(f32[16,1024]{1,0:T(8,128)S(1)} %add.70), channel_id=1, source_target_pairs={{0,4},{1,5},{2,6},{3,7},{4,0},{5,1},{6,2},{7,3},{8,12},{9,13},{10,... | collective-permute-start | bytes 196616 | tf_op jit(solution)/shard_map/ppermute | solution.py:399
  318.6 4.3 %collective-permute-start.3 = (f32[16,1024]{1,0:T(8,128)S(1)}, f32[16,1024]{1,0:T(8,128)S(1)}, u32[]{:S(2)}, u32[]{:S(2)}) collective-permute-start(f32[16,1024]{1,0:T(8,128)S(1)} %add.71), channel_id=1, source_target_pairs={{0,8},{8,0},{16,24},{24,16},{1,9},{9,1},{17,25},{25,17},{2,10},{10... | collective-permute-start | bytes 196616 | tf_op jit(solution)/shard_map/ppermute | solution.py:399
  322.9 15.8 %collective-permute-start.4 = (f32[16,1024]{1,0:T(8,128)S(1)}, f32[16,1024]{1,0:T(8,128)S(1)}, u32[]{:S(2)}, u32[]{:S(2)}) collective-permute-start(f32[16,1024]{1,0:T(8,128)S(1)} %add.72), channel_id=1, source_target_pairs={{0,16},{8,24},{16,0},{24,8},{1,17},{9,25},{17,1},{25,9},{2,18},{10... | collective-permute-start | bytes 196616 | tf_op jit(solution)/shard_map/ppermute | solution.py:399
Sparse Core Ops, SparseCore 0:
  10.9 80.0 all-gather.2
  93.9 113.4 all-gather.4

commit v2 on v1

--- a/solution.py
+++ b/solution.py
@@ -47,59 +47,104 @@
     return pltpu.CompilerParams(vmem_limit_bytes=VMEM_LIMIT)
 
 
-def attn_fwd_kernel(n_ref, w_ref, e_ref, lr_ref, kaug_ref, qaug_ref, bias_ref, qkv_ref, o_ref, lse_ref):
-    rows = n_ref.shape[0]
-    w = w_ref[0].reshape(384, w_ref.shape[3])
-    res = dot_nt(w, n_ref[...]) + dot_nn(e_ref[0], lr_ref[...])
-    low = res.astype(bf16)
+def cost(us):
+    return pl.CostEstimate(flops=int(us * 1e9), bytes_accessed=int(us * 2e6), transcendentals=0)
+
+
+def pipeline(number, *stages):
+    held = {}
+    for t in range(number + len(stages) - 1):
+        for k, stage in enumerate(stages):
+            unit = t - k
+            if 0 <= unit < number:
+                held[unit] = stage(unit, *held.pop(unit, ()))
+
+
+def score_block(ka, qa, bias_ref, ib):
+    s = dot_tn(ka[:, : (ib + 1) * BLOCK], qa[:, ib * BLOCK : (ib + 1) * BLOCK])
+    diag = s[ib * BLOCK :] + bias_ref[ib]
+    return jnp.concatenate([s[: ib * BLOCK], diag], axis=0) if ib else diag
+
+
+def attn_fwd_kernel(ids_ref, n_ref, w0_ref, w1_ref, w2_ref, w3_ref, e_ref, lr_ref, kaug_ref, qaug_ref, bias_ref, *refs):
+    qkv_ref, o_ref, lse_ref, w_ref, wo_ref, tick_ref = refs[-6:]
+    tick_ref[...] = jnp.zeros_like(tick_ref)
+    rows, width = n_ref.shape
+    pieces = [ref[...].reshape(128, width) for ref in (w0_ref, w1_ref, w2_ref, w3_ref)]
+    w = jnp.concatenate([p[:96] for p in pieces], axis=0)
+    w_ref[0] = w
+    wo_ref[0] = jnp.concatenate([p[96:] for p in pieces], axis=0)
+    e = jnp.concatenate([e_ref[0, ids_ref[r]] for r in range(4)], axis=0)
+    low = (dot_nt(w, n_ref[...]) + dot_nn(e, lr_ref[...])).astype(bf16)
+    heads = []
     for h in range(2):
         a, b = h * 192, h * 192 + 96
         q = jnp.concatenate([low[a : a + 32], low[b : b + 32]], axis=0) * bf16(0.125)
         k = jnp.concatenate([low[a + 32 : a + 64], low[b + 32 : b + 64]], axis=0)
         v = jnp.concatenate([low[a + 64 : a + 96], low[b + 64 : b + 96]], axis=0)
-        qkv_ref[0, h * 192 : h * 192 + 64] = q
-        qkv_ref[0, h * 192 + 64 : h * 192 + 128] = k
-        qkv_ref[0, h * 192 + 128 : h * 192 + 192] = v
-        qa = jnp.concatenate([q, qaug_ref[...]], axis=0)
-        ka = jnp.concatenate([k, kaug_ref[...]], axis=0)
-        for ib in range(rows // BLOCK):
-            here = slice(ib * BLOCK, (ib + 1) * BLOCK)
-            upto = (ib + 1) * BLOCK
-            s = dot_tn(ka[:, :upto], qa[:, here])
-            diag = s[ib * BLOCK :] + bias_ref[ib]
-            s = jnp.concatenate([s[: ib * BLOCK], diag], axis=0) if ib else diag
-            top = jnp.max(s, axis=0, keepdims=True)
-            p = jnp.exp(s - top)
-            total = jnp.sum(p, axis=0, keepdims=True)
-            o = dot_nn(v[:, :upto], p.astype(bf16)) * (1.0 / total)
-            o_ref[0, h * 64 : (h + 1) * 64, here] = o.astype(bf16)
-            lse_ref[0, h : h + 1, here] = top + jnp.log(total)
-
-
-def attn_fwd(normed, w, e, lr, kaug, qaug, bias):
-    shards = w.shape[0]
+        for t, part in enumerate((q, k, v)):
+            qkv_ref[0, h * 192 + t * 64 : h * 192 + t * 64 + 64] = part
+        heads.append((jnp.concatenate([q, qaug_ref[...]], axis=0), jnp.concatenate([k, kaug_ref[...]], axis=0), v))
+    units = [(h, ib) for ib in range(rows // BLOCK) for h in range(2)]
+
+    def scores(t):
+        h, ib = units[t]
+        return (score_block(heads[h][1], heads[h][0], bias_ref, ib),)
+
+    def softmax(t, s):
+        h, ib = units[t]
+        top = jnp.max(s, axis=0, keepdims=True)
+        p = jnp.exp(s - top)
+        total = jnp.sum(p, axis=0, keepdims=True)
+        lse_ref[0, h : h + 1, ib * BLOCK : (ib + 1) * BLOCK] = top + jnp.log(total)
+        return p.astype(bf16), 1.0 / total
+
+    def attend(t, p, share):
+        h, ib = units[t]
+        o = dot_nn(heads[h][2][:, : (ib + 1) * BLOCK], p) * share
+        o_ref[0, h * 64 : (h + 1) * 64, ib * BLOCK : (ib + 1) * BLOCK] = o.astype(bf16)
+
+    pipeline(len(units), scores, softmax, attend)
+
+
+def attn_fwd(ids, normed, pieces, e, lr, kaug, qaug, bias, first, number, shards, kept=None):
     rows, width = normed.shape
-    return pl.pallas_call(
+    one = len(pieces) == 1
+
+    def piece(r):
+        if one:
+            return pl.BlockSpec((1, 1, 128, width), lambda i, ids: (i, ids[r], 0, 0))
+        return pl.BlockSpec((1, 128, width), lambda i, ids: (i, 0, 0))
+
+    def fixed(a):
+        return pl.BlockSpec(a.shape, lambda i, ids: (0,) * a.ndim)
+
+    def placed(*shape):
+        return pl.BlockSpec((1,) + shape, lambda i, ids: (first + i,) + (0,) * len(shape))
+
+    shapes = [((384, rows), bf16), ((128, rows), bf16), ((2, rows), f32), ((384, width), bf16), ((128, width), bf16)]
+    tick = jax.ShapeDtypeStruct((8, 128), f32)
+    kept = [] if kept is None else list(kept)
+    *kept, tick = pl.pallas_call(
         attn_fwd_kernel,
-        grid=(shards,),
-        in_specs=[
-            whole(normed),
-            pl.BlockSpec((1, 4, 96, width), lambda i: (i, 0, 0, 0)),
-            pl.BlockSpec((1,) + e.shape[1:], lambda i: (i, 0, 0)),
-            whole(lr), whole(kaug), whole(qaug), whole(bias),
-        ],
-        out_specs=[
-            pl.BlockSpec((1, 384, rows), lambda i: (i, 0, 0)),
-            pl.BlockSpec((1, 128, rows), lambda i: (i, 0, 0)),
-            pl.BlockSpec((1, 2, rows), lambda i: (i, 0, 0)),
-        ],
-        out_shape=[
-            jax.ShapeDtypeStruct((shards, 384, rows), bf16),
-            jax.ShapeDtypeStruct((shards, 128, rows), bf16),
-            jax.ShapeDtypeStruct((shards, 2, rows), f32),
-        ],
+        grid_spec=pltpu.PrefetchScalarGridSpec(
+            num_scalar_prefetch=1,
+            grid=(number,),
+            in_specs=[fixed(normed)]
+            + [piece(r) for r in range(4)]
+            + [
+                pl.BlockSpec((1,) + e.shape[1:], lambda i, ids: (ids[4 + first + i], 0, 0, 0)),
+                fixed(lr), fixed(kaug), fixed(qaug), fixed(bias),
+            ]
+            + [pl.BlockSpec(memory_space=pl.ANY) for _ in kept],
+            out_specs=[placed(*shape) for shape, _ in shapes] + [fixed(tick)],
+        ),
+        out_shape=[jax.ShapeDtypeStruct((shards,) + shape, kind) for shape, kind in shapes] + [tick],
+        input_output_aliases={11 + t: t for t in range(len(kept))},
         compiler_params=params(),
-    )(normed, w, e, lr, kaug, qaug, bias)
+        cost_estimate=cost(2 + 4 * number),
+    )(ids, normed, *(pieces * 4 if one else pieces), e, lr, kaug, qaug, bias, *kept)
+    return kept, tick
 
 
 def norm_stats(v):
@@ -129,125 +174,167 @@
     return pl.pallas_call(
         out_proj_kernel,
         grid=(rows // BLOCK,),
-        in_specs=[
-            pl.BlockSpec((shards, 128, BLOCK), lambda i: (0, 0, i)),
-            pl.BlockSpec((shards, 4, 32, width), lambda i: (0, 0, 3, 0)),
-            blk,
-            whole(gain),
-        ],
+        in_specs=[pl.BlockSpec((shards, 128, BLOCK), lambda i: (0, 0, i)), whole(w), blk, whole(gain)],
         out_specs=[blk, blk],
         out_shape=[jax.ShapeDtypeStruct((rows, width), f32), jax.ShapeDtypeStruct((rows, width), bf16)],
         compiler_params=params(),
+        cost_estimate=cost(7),
     )(o, w, x, gain)
 
 
 GELU_C = math.sqrt(2.0 / math.pi)
 
 
-def mlp_kernel(n_ref, g_ref, b_ref, mid_ref, valid_ref, gain_ref, wo_ref, out_ref, gmid_ref, do_ref, mlp_acc, gnt_acc, *, chunk):
+def mlp_kernel(ids_ref, n_ref, g_ref, *refs, sources, resumed, last):
+    pieces, refs = refs[:sources], refs[sources:]
+    if resumed:
+        mlp_in, gnt_in, refs = refs[0], refs[1], refs[2:]
+    if last:
+        mid_ref, valid_ref, gain_ref, wo_ref, out_ref, gmid_ref, do_ref, mlp_acc, gnt_acc, sems = refs
+    else:
+        mlp_acc, gnt_acc, sems = refs
     step = pl.program_id(0)
     rows, width = n_ref.shape
 
     @pl.when(step == 0)
     def _():
-        mlp_acc[...] = jnp.zeros_like(mlp_acc)
-        gnt_acc[...] = jnp.zeros_like(gnt_acc)
-
-    up = b_ref[0, :, :128].reshape(512, width)
-    down = b_ref[0, :, 128:].reshape(512, width)
-
-    @pl.loop(0, rows // chunk)
-    def _(c):
-        at = pl.ds(pl.multiple_of(c * chunk, chunk), chunk)
-        u = dot_nt(n_ref[at, :], up)
-        gh = dot_nt(g_ref[at, :], down)
-        uu = u * u
-        th = jnp.tanh(u * (GELU_C + (GELU_C * 0.044715) * uu))
-        half = 0.5 + 0.5 * th
-        hidden = u * half
-        slope = half + (0.5 * u) * (1.0 - th * th) * (GELU_C + (3.0 * 0.044715 * GELU_C) * uu)
-        mlp_acc[at, :] += dot_nn(hidden.astype(bf16), down)
-        gnt_acc[at, :] += dot_nn((gh * slope).astype(bf16), up)
-
-    @pl.when(step == pl.num_programs(0) - 1)
-    def _():
-        wo = wo_ref[...].reshape(width, width)
-
-        @pl.loop(0, rows // BLOCK)
-        def _(c):
-            at = pl.ds(pl.multiple_of(c * BLOCK, BLOCK), BLOCK)
-            mid = mid_ref[at, :]
-            out_ref[at, :] = ((mid + mlp_acc[at, :]) * valid_ref[at, :]).astype(bf16)
-            n, r = norm_stats(mid)
-            gmid = g_ref[at, :].astype(f32) + norm_back(n, r, gnt_acc[at, :] * gain_ref[...])
-            gmid_ref[at, :] = gmid
-            do_ref[:, :, at] = dot_nt(wo, gmid.astype(bf16)).astype(bf16).reshape(do_ref.shape[0], 128, BLOCK)
-
-
-def mlp(normed, g, b, mid, valid, gain, a, chunk=512):
+        if resumed:
+            copies = [
+                pltpu.make_async_copy(src, dst, sems.at[t])
+                for t, (src, dst) in enumerate(((mlp_in, mlp_acc), (gnt_in, gnt_acc)))
+            ]
+            for c in copies:
+                c.start()
+            for c in copies:
+                c.wait()
+        else:
+            mlp_acc[...] = jnp.zeros_like(mlp_acc)
+            gnt_acc[...] = jnp.zeros_like(gnt_acc)
+
+    held = [ref[...].reshape(-1, 128, width) for ref in pieces]
+    up = jnp.concatenate([p[:, :64].reshape(-1, width) for p in held], axis=0)
+    down = jnp.concatenate([p[:, 64:].reshape(-1, width) for p in held], axis=0)
+    u = dot_nt(n_ref[...], up)
+    gh = dot_nt(g_ref[...], down)
+    uu = u * u
+    th = jnp.tanh(u * (GELU_C + (GELU_C * 0.044715) * uu))
+    half = 0.5 + 0.5 * th
+    hidden = u * half
+    slope = half + (0.5 * u) * (1.0 - th * th) * (GELU_C + (3.0 * 0.044715 * GELU_C) * uu)
+    mlp_acc[...] += dot_nn(hidden.astype(bf16), down)
+    gnt_acc[...] += dot_nn((gh * slope).astype(bf16), up)
+
+    if last:
+
+        @pl.when(step == pl.num_programs(0) - 1)
+        def _():
+            wo = wo_ref[...].reshape(width, width)
+
+            @pl.loop(0, rows // BLOCK)
+            def _(c):
+                at = pl.ds(pl.multiple_of(c * BLOCK, BLOCK), BLOCK)
+                mid = mid_ref[at, :]
+                out_ref[at, :] = ((mid + mlp_acc[at, :]) * valid_ref[at, :]).astype(bf16)
+                n, r = norm_stats(mid)
+                gmid = g_ref[at, :].astype(f32) + norm_back(n, r, gnt_acc[at, :] * gain_ref[...])
+                gmid_ref[at, :] = gmid
+                do_ref[:, :, at] = dot_nt(wo, gmid.astype(bf16)).astype(bf16).reshape(do_ref.shape[0], 128, BLOCK)
+
+
+def mlp(ids, normed, g, pieces, steps, kept=None, final=None, gathered=False):
     rows, width = normed.shape
-    shards = b.shape[0]
+    acc = jax.ShapeDtypeStruct((rows, width), f32)
+    sems = pltpu.SemaphoreType.DMA((2,))
+    kept = [] if kept is None else list(kept)
+
+    def fixed(a):
+        return pl.BlockSpec(a.shape, lambda i, ids: (0,) * len(a.shape))
+
+    def taken(t, a):
+        if gathered:
+            return pl.BlockSpec((1,) + a.shape[1:], lambda i, ids: (ids[6 + len(pieces) * i + t],) + (0,) * (a.ndim - 1))
+        return pl.BlockSpec((a.shape[0] // steps,) + a.shape[1:], lambda i, ids: (i,) + (0,) * (a.ndim - 1))
+
+    if final is None:
+        extra, out_shape, scratch = [], [acc, acc], [sems]
+    else:
+        extra = list(final)
+        shards = extra[3].shape[0]
+        out_shape = [
+            jax.ShapeDtypeStruct((rows, width), bf16),
+            acc,
+            jax.ShapeDtypeStruct((shards, 128, rows), bf16),
+        ]
+        scratch = [pltpu.VMEM((rows, width), f32)] * 2 + [sems]
     return pl.pallas_call(
-        functools.partial(mlp_kernel, chunk=chunk),
-        grid=(shards,),
-        in_specs=[
-            whole(normed), whole(g),
-            pl.BlockSpec((1,) + b.shape[1:], lambda i: (i, 0, 0, 0)),
-            whole(mid), whole(valid), whole(gain),
-            pl.BlockSpec((shards, 4, 32, width), lambda i: (0, 0, 3, 0)),
-        ],
-        out_specs=[
-            pl.BlockSpec((rows, width), lambda i: (0, 0)),
-            pl.BlockSpec((rows, width), lambda i: (0, 0)),
-            pl.BlockSpec((shards, 128, rows), lambda i: (0, 0, 0)),
-        ],
-        out_shape=[
-            jax.ShapeDtypeStruct((rows, width), bf16),
-            jax.ShapeDtypeStruct((rows, width), f32),
-            jax.ShapeDtypeStruct((shards, 128, rows), bf16),
-        ],
-        scratch_shapes=[pltpu.VMEM((rows, width), f32)] * 2,
+        functools.partial(mlp_kernel, sources=len(pieces), resumed=bool(kept), last=final is not None),
+        grid_spec=pltpu.PrefetchScalarGridSpec(
+            num_scalar_prefetch=1,
+            grid=(steps,),
+            in_specs=[fixed(normed), fixed(g)]
+            + [taken(t, a) for t, a in enumerate(pieces)]
+            + [pl.BlockSpec(memory_space=pl.ANY) for _ in kept]
+            + [fixed(a) for a in extra],
+            out_specs=[fixed(a) for a in out_shape],
+            scratch_shapes=scratch,
+        ),
+        out_shape=out_shape,
         compiler_params=params(),
-    )(normed, g, b, mid, valid, gain, a)
-
-
-def attn_bwd_kernel(qkv_ref, o_ref, do_ref, lse_ref, kaug_ref, qaug_ref, bias_ref, et_ref, lrs_ref, dqkv_ref, gl_ref, gb_ref, dk_acc, dv_acc):
+        cost_estimate=cost(4 + 5 * steps),
+    )(ids, normed, g, *pieces, *kept, *extra)
+
+
+def attn_bwd_kernel(ids_ref, qkv_ref, o_ref, do_ref, lse_ref, kaug_ref, qaug_ref, bias_ref, et_ref, lrs_ref, n_ref, d_ref, gl_ref, sum_ref, dk_acc, dv_acc, gb_acc):
     rows = qkv_ref.shape[2]
     step = pl.program_id(0)
+    heads = []
+    for h in range(2):
+        q, k, v = (qkv_ref[0, h * 192 + 64 * t : h * 192 + 64 * t + 64] for t in range(3))
+        heads.append((q, k, v, jnp.concatenate([q, qaug_ref[...]], axis=0), jnp.concatenate([k, kaug_ref[...]], axis=0)))
+    units = [(h, ib) for h in range(2) for ib in range(rows // BLOCK)]
+
+    def products(t):
+        h, ib = units[t]
+        q, k, v, qa, ka = heads[h]
+        here = slice(ib * BLOCK, (ib + 1) * BLOCK)
+        do, o = (ref[0, h * 64 : (h + 1) * 64, here] for ref in (do_ref, o_ref))
+        inner = jnp.sum(do.astype(f32) * o.astype(f32), axis=0, keepdims=True)
+        return do, inner, score_block(ka, qa, bias_ref, ib), dot_tn(v[:, : (ib + 1) * BLOCK], do)
+
+    def scores(t, do, inner, s, dp):
+        h, ib = units[t]
+        p = jnp.exp(s - lse_ref[0, h : h + 1, ib * BLOCK : (ib + 1) * BLOCK])
+        return do, (p * (dp - inner)).astype(bf16), p.astype(bf16)
+
+    def grads(t, do, ds, p):
+        h, ib = units[t]
+        c = h * 192
+        q, k = heads[h][:2]
+        before, here = slice(0, ib * BLOCK), slice(ib * BLOCK, (ib + 1) * BLOCK)
+        dq = (dot_nn(k[:, : (ib + 1) * BLOCK], ds) * 0.125).astype(bf16)
+        d_ref[0, c : c + 32, here] = dq[:32]
+        d_ref[0, c + 96 : c + 128, here] = dq[32:]
+        for acc, part in ((dk_acc, dot_nt(q[:, here], ds)), (dv_acc, dot_nt(do, p))):
+            if ib:
+                acc[h, :, before] += part[:, before]
+            acc[h, :, here] = part[:, here]
+
+    pipeline(len(units), products, scores, grads)
     for h in range(2):
         c = h * 192
-        q, k, v = (qkv_ref[0, c + 64 * t : c + 64 * t + 64] for t in range(3))
-        qa = jnp.concatenate([q, qaug_ref[...]], axis=0)
-        ka = jnp.concatenate([k, kaug_ref[...]], axis=0)
-        for ib in range(rows // BLOCK):
-            here = slice(ib * BLOCK, (ib + 1) * BLOCK)
-            upto = (ib + 1) * BLOCK
-            do = do_ref[0, h * 64 : (h + 1) * 64, here]
-            o = o_ref[0, h * 64 : (h + 1) * 64, here]
-            inner = jnp.sum(do.astype(f32) * o.astype(f32), axis=0, keepdims=True)
-            s = dot_tn(ka[:, :upto], qa[:, here])
-            diag = s[ib * BLOCK :] + bias_ref[ib]
-            s = jnp.concatenate([s[: ib * BLOCK], diag], axis=0) if ib else diag
-            p = jnp.exp(s - lse_ref[0, h : h + 1, here])
-            dp = dot_tn(v[:, :upto], do)
-            ds = (p * (dp - inner)).astype(bf16)
-            pb = p.astype(bf16)
-            dq = (dot_nn(k[:, :upto], ds) * 0.125).astype(bf16)
-            dqkv_ref[0, c : c + 32, here] = dq[:32]
-            dqkv_ref[0, c + 96 : c + 128, here] = dq[32:]
-            dk = dot_nt(q[:, here], ds)
-            dv = dot_nt(do, pb)
-            if ib:
-                dk_acc[:, : ib * BLOCK] += dk[:, : ib * BLOCK]
-                dv_acc[:, : ib * BLOCK] += dv[:, : ib * BLOCK]
-            dk_acc[:, here] = dk[:, ib * BLOCK :]
-            dv_acc[:, here] = dv[:, ib * BLOCK :]
         for t, acc in ((32, dk_acc), (64, dv_acc)):
-            low = acc[...].astype(bf16)
-            dqkv_ref[0, c + t : c + t + 32] = low[:32]
-            dqkv_ref[0, c + 96 + t : c + 128 + t] = low[32:]
-    d = dqkv_ref[0]
-    gl = dot_nn(et_ref[0], d)
+            low = acc[h].astype(bf16)
+            d_ref[0, c + t : c + t + 32] = low[:32]
+            d_ref[0, c + 96 + t : c + 128 + t] = low[32:]
+    gl = jnp.zeros((16, rows), f32)
+    shard = ids_ref[4 + step]
+    for r in range(4):
+        d = d_ref[0, r * 96 : r * 96 + 96]
+        gl += dot_nn(et_ref[0, ids_ref[r]], d)
+        gb = dot_nt(lrs_ref[...], d)
+        gb = adapter_scale * (gb[:8] + gb[8:])
+        is_query = lax.broadcasted_iota(jnp.int32, (8, 32), 0) < 4
+        gb_acc[shard * 4 + ids_ref[r]] = jnp.where(is_query, gb[:, :32], gb[:, 64:96])
     gl = gl[:8] + gl[8:]
 
     @pl.when(step == 0)
@@ -258,53 +345,48 @@
     def _():
         gl_ref[...] += gl
 
-    gb = dot_nt(lrs_ref[...], d)
-    gb_ref[0] = gb[:8] + gb[8:]
-
-
-def attn_bwd(qkv, o, do, lse, kaug, qaug, bias, et, lrs):
+    @pl.when(step == pl.num_programs(0) - 1)
+    def _():
+        hi, lo = split_hi_lo(gl_ref[...])
+        sum_ref[:8] = dot_nn(hi, n_ref[...]) + dot_nn(lo, n_ref[...])
+        sum_ref[8:] = jnp.concatenate([gb_acc[t] for t in range(gb_acc.shape[0])], axis=1)
+
+
+def attn_bwd(ids, qkv, o, do, lse, kaug, qaug, bias, et, lrs, normed):
     shards, _, rows = qkv.shape
+    width = normed.shape[1]
+
+    def fixed(*shape):
+        return pl.BlockSpec(shape, lambda i, ids: (0,) * len(shape))
+
+    def rel(*shape):
+        return pl.BlockSpec((1,) + shape, lambda i, ids: (i,) + (0,) * len(shape))
+
     return pl.pallas_call(
         attn_bwd_kernel,
-        grid=(shards,),
-        in_specs=[
-            pl.BlockSpec((1, 384, rows), lambda i: (i, 0, 0)),
-            pl.BlockSpec((1, 128, rows), lambda i: (i, 0, 0)),
-            pl.BlockSpec((1, 128, rows), lambda i: (i, 0, 0)),
-            pl.BlockSpec((1, 2, rows), lambda i: (i, 0, 0)),
-            whole(kaug), whole(qaug), whole(bias),
-            pl.BlockSpec((1, 16, 384), lambda i: (i, 0, 0)),
-            whole(lrs),
-        ],
-        out_specs=[
-            pl.BlockSpec((1, 384, rows), lambda i: (i, 0, 0)),
-            pl.BlockSpec((8, rows), lambda i: (0, 0)),
-            pl.BlockSpec((1, 8, 384), lambda i: (i, 0, 0)),
-        ],
+        grid_spec=pltpu.PrefetchScalarGridSpec(
+            num_scalar_prefetch=1,
+            grid=(shards,),
+            in_specs=[
+                rel(384, rows), rel(128, rows), rel(128, rows), rel(2, rows),
+                fixed(*kaug.shape), fixed(*qaug.shape), fixed(*bias.shape),
+                pl.BlockSpec((1,) + et.shape[1:], lambda i, ids: (ids[4 + i], 0, 0, 0)),
+                fixed(*lrs.shape), fixed(*normed.shape),
+            ],
+            out_specs=[rel(384, rows), fixed(8, rows), fixed(16, width)],
+            scratch_shapes=[pltpu.VMEM((2, 64, rows), f32)] * 2 + [pltpu.VMEM((4 * shards, 8, 32), f32)],
+        ),
         out_shape=[
             jax.ShapeDtypeStruct((shards, 384, rows), bf16),
             jax.ShapeDtypeStruct((8, rows), f32),
-            jax.ShapeDtypeStruct((shards, 8, 384), f32),
+            jax.ShapeDtypeStruct((16, width), f32),
         ],
-        scratch_shapes=[pltpu.VMEM((64, rows), f32)] * 2,
         compiler_params=params(),
-    )(qkv, o, do, lse, kaug, qaug, bias, et, lrs)
-
-
-def grad_a_kernel(gl_ref, n_ref, out_ref):
-    hi, lo = split_hi_lo(gl_ref[...])
-    out_ref[...] = dot_nn(hi, n_ref[...]) + dot_nn(lo, n_ref[...])
-
-
-def grad_a_rows(gl, normed):
-    return pl.pallas_call(
-        grad_a_kernel,
-        out_shape=jax.ShapeDtypeStruct((8, normed.shape[1]), f32),
-        compiler_params=params(),
-    )(gl, normed)
-
-
-def input_grad_kernel(d_ref, w_ref, gl_ref, dn_ref, x_ref, gmid_ref, gain_ref, out_ref):
+        cost_estimate=cost(35),
+    )(ids, qkv, o, do, lse, kaug, qaug, bias, et, lrs, normed)
+
+
+def input_grad_kernel(d_ref, w_ref, gl_ref, dn_ref, x_ref, gmid_ref, gain_ref, event_ref, out_ref):
     width = x_ref.shape[1]
     d = d_ref[...].reshape(-1, BLOCK)
     w = w_ref[...].reshape(-1, width)
@@ -316,7 +398,7 @@
     out_ref[...] = (gmid_ref[...] + norm_back(n, r, g * gain_ref[...])).astype(bf16)
 
 
-def input_grad_rows(d, w, gl, down_t, x, gmid, gain):
+def input_grad_rows(d, w, gl, down_t, x, gmid, gain, event):
     rows, width = x.shape
     shards = d.shape[0]
     blk = pl.BlockSpec((BLOCK, width), lambda i: (i, 0))
@@ -325,16 +407,18 @@
         grid=(rows // BLOCK,),
         in_specs=[
             pl.BlockSpec((shards, 384, BLOCK), lambda i: (0, 0, i)),
-            pl.BlockSpec((shards, 4, 96, width), lambda i: (0, 0, 0, 0)),
+            whole(w),
             pl.BlockSpec((8, BLOCK), lambda i: (0, i)),
             whole(down_t),
             blk, blk,
             whole(gain),
+            pl.BlockSpec(memory_space=pl.ANY),
         ],
         out_specs=blk,
         out_shape=jax.ShapeDtypeStruct((rows, width), bf16),
         compiler_params=params(),
-    )(d, w, gl, down_t, x, gmid, gain)
+        cost_estimate=cost(13),
+    )(d, w, gl, down_t, x, gmid, gain, event)
 
 
 def bucket_table():
@@ -393,12 +477,12 @@
     return hi.astype(bf16), (v - hi).astype(bf16)
 
 
-def xor_sum(v, axis, size):
-    step = 1
-    while step < size:
-        v = v + lax.ppermute(v, axis, [(i, i ^ step) for i in range(size)])
-        step *= 2
-    return v
+def flip_send(v, axis, bits):
+    return lax.ppermute(v, axis, [(i, i ^ bits) for i in range(lax.axis_size(axis))])
+
+
+def flip_sum(v, axis, flips):
+    return sum([flip_send(v, axis, k) for k in flips], v)
 
 
 def whole_item_shards(
@@ -424,13 +508,37 @@
     model_index = lax.axis_index("mp")
     group_index = lax.axis_index("dp")
     shards = mp_size
-    qkv_t = jnp.transpose(query_key_value_weight.reshape(width, 2, 3, 2, 32), (1, 3, 2, 4, 0)).reshape(4, 96, width)
-    a_own = jnp.concatenate([qkv_t, output_matrix.reshape(4, 32, width)], axis=1)
-    b_own = jnp.concatenate([up_matrix.reshape(4, 128, width), down_matrix.reshape(4, 128, width)], axis=1)
-    a_piece = lax.dynamic_slice_in_dim(a_own, group_index, 1, 0)
-    b_piece = lax.dynamic_slice_in_dim(b_own, group_index, 1, 0)
-    a_all = lax.all_gather(a_piece, ("mp", "dp"), axis=0, tiled=True).reshape(shards, 4, 128, width)
-    b_all = lax.all_gather(b_piece, ("mp", "dp"), axis=0, tiled=True).reshape(shards, 4, 256, width)
+    qkv_own = jnp.transpose(query_key_value_weight.reshape(width, 2, 3, 2, 32), (1, 3, 2, 4, 0))
+    a_own = jnp.concatenate([qkv_own.reshape(4, 96, width), output_matrix.reshape(4, 32, width)], axis=1)
+    b_own = jnp.concatenate([up_matrix.reshape(4, 2, 64, width), down_matrix.reshape(4, 2, 64, width)], axis=2)
+
+    def after(v, *events):
+        return lax.optimization_barrier((v,) + events)[0]
+
+    def quarter(own):
+        return lax.dynamic_slice_in_dim(own, group_index, 1, 0)
+
+    def across(v, flips):
+        return jnp.concatenate([flip_send(v, "mp", k) for k in flips], axis=0)
+
+    def plane(v):
+        return [v] + [flip_send(v, "dp", k) for k in range(1, dp_size)]
+
+    def other_core(arrays):
+        return [flip_send(a, "mp", 1) for a in arrays]
+
+    b_gathered = lax.all_gather(quarter(b_own), ("mp", "dp"), axis=0, tiled=True).reshape(shards, 8, 128, width)
+    (a_core,) = other_core([a_own])
+    a_far = across(quarter(a_own), (4, 6))
+    a_near = flip_send(a_own, "mp", 2)
+    (b_core,) = other_core([after(b_own, a_core)])
+    (a_near_core,) = other_core([a_near])
+    ids = jnp.concatenate(
+        [
+            group_index ^ jnp.arange(4, dtype=jnp.int32),
+            model_index ^ jnp.array([0, 1, 2, 3, 4, 6, 5, 7], dtype=jnp.int32),
+        ]
+    )
 
     valid_all = token_valid(counts[0], lengths[0])
     valid = lax.dynamic_slice_in_dim(valid_all, model_index * rows, rows)
@@ -459,24 +567,34 @@
     zero = jnp.zeros_like(qu)
     factor = jnp.concatenate(
         [jnp.concatenate([qu, zero, zero], axis=3), jnp.concatenate([zero, zero, vu], axis=3)], axis=0
-    ).reshape(8, shards, 384)
+    ).reshape(8, shards, 4, 96)
     fhi, flo = exact_hi_lo(factor)
-    e = jnp.transpose(jnp.concatenate([fhi, fhi, flo, jnp.zeros_like(fhi)], axis=0), (1, 2, 0))
-    et = jnp.transpose(jnp.concatenate([fhi, flo], axis=0), (1, 0, 2))
+    e = jnp.transpose(jnp.concatenate([fhi, fhi, flo, jnp.zeros_like(fhi)], axis=0), (1, 2, 3, 0))
+    et = jnp.transpose(jnp.concatenate([fhi, flo], axis=0), (1, 2, 0, 3))
 
     gain_one = first_norm_gain[None, :]
     gain_two = second_norm_gain[None, :]
-    qkv, attended, lse = attn_fwd(normed, a_all, e, lr, kaug, qaug, bias)
-    mid, normed_two = out_proj(attended, a_all, tokens, gain_two)
-    output, grad_mid, grad_attended = mlp(normed_two, grad_out_low, b_all, mid, valid_col, gain_two, a_all)
-    d, gl, gb = attn_bwd(qkv, attended, grad_attended, lse, kaug, qaug, bias, et, lrs)
-    ga = grad_a_rows(gl, normed)
-    gb = gb.reshape(shards, 2, 4, 4, 3, 32)
-    gbq = jnp.transpose(gb[:, 0, :, :, 0], (1, 0, 2, 3)).reshape(4, width)
-    gbv = jnp.transpose(gb[:, 1, :, :, 2], (1, 0, 2, 3)).reshape(4, width)
-    packed = jnp.concatenate([ga, adapter_scale * gbq, adapter_scale * gbv], axis=0)
-    packed = xor_sum(xor_sum(packed, "mp", mp_size), "dp", dp_size)
-    input_grad = input_grad_rows(d, a_all, gl, down_t, tokens, grad_mid, gain_one)
+    fixed = (e, lr, kaug, qaug, bias)
+    kept, _ = attn_fwd(ids, normed, [a_own[None]], *fixed, 0, 1, shards)
+    kept, tick = attn_fwd(ids, normed, [a_core[None]], *fixed, 1, 1, shards, kept)
+    a_same = plane(after(a_far, tick))
+    kept, _ = attn_fwd(ids, normed, [a_near[None]], *fixed, 2, 1, shards, kept)
+    kept, tick = attn_fwd(ids, normed, [a_near_core[None]], *fixed, 3, 1, shards, kept)
+    a_other = other_core([after(a, tick) for a in a_same])
+    kept, _ = attn_fwd(ids, normed, a_same, *fixed, 4, 2, shards, kept)
+    kept, _ = attn_fwd(ids, normed, a_other, *fixed, 6, 2, shards, kept)
+    qkv, attended, lse, w_all, wo_all = kept
+    mid, normed_two = out_proj(attended, wo_all, tokens, gain_two)
+    sums = mlp(ids, normed_two, grad_out_low, [b_own.reshape(8, 128, width), b_core.reshape(8, 128, width)], 2)
+    output, grad_mid, grad_attended = mlp(
+        ids, normed_two, grad_out_low, [b_gathered], 6, sums, (mid, valid_col, gain_two, wo_all), gathered=True
+    )
+    d, gl, packed = attn_bwd(ids, qkv, attended, grad_attended, lse, kaug, qaug, bias, et, lrs, normed)
+    packed = flip_sum(packed, "mp", (1,))
+    packed = flip_sum(packed, "mp", (2, 4, 6))
+    event = packed
+    packed = flip_sum(packed, "dp", tuple(range(1, dp_size)))
+    input_grad = input_grad_rows(d, w_all, gl, down_t, tokens, grad_mid, gain_one, event)
     return (
         output,
         input_grad,

time: 347 us -> 272 us (0.78); the launches traced: 346 us -> 268 us
  waiting for transfers between devices: 142 us -> 33.6 us
  starting transfers between devices: 5.27 us -> 19.4 us
  Pallas kernels: 159 us -> 167 us
  other arithmetic: 17.3 us -> 22.4 us
    all_gather x2 -> x1, waiting for transfers between devices: 130 us -> 5.96 us  [whole_item_shards(): lax.all_gather(quarter(b_own), ('mp', 'dp'), axis=0, tiled=True)]
    ppermute x5 -> x20, waiting for transfers between devices: 12.1 us -> 27.7 us  [flip_send(): lax.ppermute(v, axis, [(i, i ^ bits) for i in range(lax.axis_size(axis))])]
    ppermute x5 -> x20, starting transfers between devices: 5.19 us -> 19.4 us  [flip_send(): lax.ppermute(v, axis, [(i, i ^ bits) for i in range(lax.axis_size(axis))])]
    pallas_call x4 -> x9, Pallas kernels: 138 us -> 145 us  [the longest x2 62.8 us: mlp(): pl.pallas_call(functools.partial(mlp_kernel, sources=len(pieces), resumed...]
  transfers between devices with their start and end apart: 7 -> 21, of which waited for: 6 -> 6; matrix products, arithmetic and copies ran while one was open for 5% -> 9% of each run, Pallas kernels for 18% -> 32%
where the time goes in v2:
time: 272 us; the launch traced here: 268 us
  Pallas kernels  167 us (61%)
  waiting for transfers between devices  33.6 us (12%)
  other arithmetic  22.4 us (8%)
  starting transfers between devices  19.4 us (7%)
  between operations  15 us (6%)
  local copies, waits for them, and re-layouts  9.99 us (4%)
    pallas_call x2, Pallas kernels, mlp(): pl.pallas_call(functools.partial(mlp_kernel, sources=len(pieces), resumed...  62.8 us
    pallas_call x6, Pallas kernels, attn_fwd(): pl.pallas_call(attn_fwd_kernel, grid_spec=pltpu.PrefetchScalarGridSpec(nu...  48.4 us
    pallas_call x1, Pallas kernels, attn_bwd(): pl.pallas_call(attn_bwd_kernel, grid_spec=pltpu.PrefetchScalarGridSpec(nu...  34.2 us
    ppermute x20, waiting for transfers between devices, flip_send(): lax.ppermute(v, axis, [(i, i ^ bits) for i in range(lax.axis_size(axis))])  27.7 us
    ppermute x20, starting transfers between devices, flip_send(): lax.ppermute(v, axis, [(i, i ^ bits) for i in range(lax.axis_size(axis))])  19.4 us
    pallas_call x1, Pallas kernels, input_grad_rows(): pl.pallas_call(input_grad_kernel, grid=(rows // BLOCK,), in_specs=[pl.Blo...  13.7 us
    pallas_call x1, Pallas kernels, out_proj(): pl.pallas_call(out_proj_kernel, grid=(rows // BLOCK,), in_specs=[pl.Block...  7.5 us
    all_gather x1, waiting for transfers between devices, whole_item_shards(): lax.all_gather(quarter(b_own), ('mp', 'dp'), axis=0, tiled=True)  5.96 us
  transfers between devices with their start and end apart: 21, of which 6 were waited for; matrix products, arithmetic and copies ran while one was open for 9% of the time, Pallas kernels for 32%

profile of v2, /device:TPU:0, one launch (start us, length us, event | category | flops | bytes accessed | tf_op | source)
XLA Modules:
  0.0 267.8 jit_solution(8792192381069586065)
XLA Ops:
  7.2 1.9 fusion.5
  9.3 1.6 fusion.32
  10.9 0.5 collective-permute-start.4
  11.4 2.6 collective-permute-start.2
  14.0 0.7 fusion.6
  14.7 2.6 collective-permute-start
  17.3 0.7 dynamic-slice_subtract_fusion
  18.1 0.6 fusion.35
  18.7 0.6 iota_compare_fusion.12
  19.5 0.7 iota_compare_fusion.11
  20.3 0.7 iota_compare_fusion.10
  21.0 0.7 iota_compare_fusion.9
  22.3 1.0 select_maximum_fusion
  23.3 1.3 reshape.228
  25.1 0.7 fusion.2
  25.8 0.5 copy-done.2
  26.3 0.7 fusion.4.n_ref
  27.0 0.6 fusion.13
  27.7 0.6 pad_maximum_fusion.4.lrs_ref
  28.4 0.7 maximum_bitcast_fusion.1.et_ref
  29.6 1.5 pad_maximum_fusion.1.refs_0_
  31.1 0.7 maximum_maximum_fusion.lr_ref
  31.8 0.7 select_convert_fusion
  32.6 1.5 and_select_fusion.bias_ref
  34.1 0.6 pad_add_fusion.ids_ref
  34.7 1.2 copy.76.e_ref
  35.9 1.0 copy.79.refs_4_
  36.9 6.8 %shard_map.199 = (bf16[8,384,1024]{2,1,0:T(8,128)(2,1)}, bf16[8,128,1024]{2,1,0:T(8,128)(2,1)}, f32[8,2,1024]{2,1,0:T(2,128)}, bf16[8,384,1024]{2,1,0:T(8,128)(2...) custom-call(s32[12]{0:T(128)} %pad_add_fusion.ids_ref, bf16[1024,1024]{1,0:T(8,128)(2,1)} %copy-done, ...), custom_call_target="tpu_custom_call" | custom-call | flops 6000000000 | bytes 12000000 | tf_op jit(solution)/shard_map/pallas_call | solution.py:128
  43.7 1.7 multiply_convert_fusion.g_ref
  45.4 9.9 %collective-permute-done = bf16[1,128,1024]{2,1,0:T(8,128)(2,1)} collective-permute-done((bf16[1,128,1024]{2,1,0:T(8,128)(2,1)}, bf16[1,128,1024]{2,1,0:T(8,128)(2,1)}, u32[]{:S(2)}, u32[]{:S(2)}) %collective-permute-start) | collective-permute-done | bytes 262176 | tf_op jit(solution)/shard_map/ppermute | solution.py:481
  55.4 12.7 %collective-permute-done.1 = bf16[1,128,1024]{2,1,0:T(8,128)(2,1)} collective-permute-done((bf16[1,128,1024]{2,1,0:T(8,128)(2,1)}, bf16[1,128,1024]{2,1,0:T(8,128)(2,1)}, u32[]{:S(2)}, u32[]{:S(2)}) %collective-permute-start.1) | collective-permute-done | bytes 262176 | tf_op jit(solution)/shard_map/ppermute | solution.py:481
  68.1 1.1 pad_maximum_fusion.3.w0_ref
  69.2 2.6 collective-permute-start.10
  71.7 0.5 collective-permute-start.6
  72.3 0.5 collective-permute-start.8
  72.7 0.5 collective-permute-start.3
  73.2 6.7 %shard_map.200 = (bf16[8,384,1024]{2,1,0:T(8,128)(2,1)}, bf16[8,128,1024]{2,1,0:T(8,128)(2,1)}, f32[8,2,1024]{2,1,0:T(2,128)}, bf16[8,384,1024]{2,1,0:T(8,128)(2...) custom-call(s32[12]{0:T(128)} %pad_add_fusion.ids_ref, ...), custom_call_target="tpu_custom_call", output_to_operand_aliasing={{0}: (11, {}), {1}: (12, {}), {2}: (13, {}), {3}: (14, {}),... | custom-call | flops 6000000000 | bytes 12000000 | tf_op jit(solution)/shard_map/pallas_call | solution.py:128
  79.9 6.7 %shard_map.201 = (bf16[8,384,1024]{2,1,0:T(8,128)(2,1)}, bf16[8,128,1024]{2,1,0:T(8,128)(2,1)}, f32[8,2,1024]{2,1,0:T(2,128)}, bf16[8,384,1024]{2,1,0:T(8,128)(2...) custom-call(s32[12]{0:T(128)} %pad_add_fusion.ids_ref, ...), custom_call_target="tpu_custom_call", output_to_operand_aliasing={{0}: (11, {}), {1}: (12, {}), {2}: (13, {}), {3}: (14, {}),... | custom-call | flops 6000000000 | bytes 12000000 | tf_op jit(solution)/shard_map/pallas_call | solution.py:128
  86.6 1.0 copy-done.4
  87.6 6.6 %shard_map.202 = (bf16[8,384,1024]{2,1,0:T(8,128)(2,1)}, bf16[8,128,1024]{2,1,0:T(8,128)(2,1)}, f32[8,2,1024]{2,1,0:T(2,128)}, bf16[8,384,1024]{2,1,0:T(8,128)(2...) custom-call(s32[12]{0:T(128)} %pad_add_fusion.ids_ref, ...), custom_call_target="tpu_custom_call", output_to_operand_aliasing={{0}: (11, {}), {1}: (12, {}), {2}: (13, {}), {3}: (14, {}),... | custom-call | flops 6000000000 | bytes 12000000 | tf_op jit(solution)/shard_map/pallas_call | solution.py:128
  94.4 0.4 collective-permute-start.9
  94.9 0.6 collective-permute-start.5
  95.6 11.5 %shard_map.203 = (bf16[8,384,1024]{2,1,0:T(8,128)(2,1)}, bf16[8,128,1024]{2,1,0:T(8,128)(2,1)}, f32[8,2,1024]{2,1,0:T(2,128)}, bf16[8,384,1024]{2,1,0:T(8,128)(2...) custom-call(s32[12]{0:T(128)} %pad_add_fusion.ids_ref, ...), custom_call_target="tpu_custom_call", output_to_operand_aliasing={{0}: (11, {}), {1}: (12, {}), {2}: (13, {}), {3}: (14, {}),... | custom-call | flops 10000000000 | bytes 20000000 | tf_op jit(solution)/shard_map/pallas_call | solution.py:128
  107.3 0.7 copy-done.22
  108.5 10.1 %shard_map.204 = (bf16[8,384,1024]{2,1,0:T(8,128)(2,1)}, bf16[8,128,1024]{2,1,0:T(8,128)(2,1)}, f32[8,2,1024]{2,1,0:T(2,128)}, bf16[8,384,1024]{2,1,0:T(8,128)(2...) custom-call(s32[12]{0:T(128)} %pad_add_fusion.ids_ref, ...), custom_call_target="tpu_custom_call", output_to_operand_aliasing={{0}: (11, {}), {1}: (12, {}), {2}: (13, {}), {3}: (14, {}),... | custom-call | flops 10000000000 | bytes 20000000 | tf_op jit(solution)/shard_map/pallas_call | solution.py:128
  118.6 7.5 %shard_map.205 = (f32[1024,1024]{1,0:T(8,128)}, bf16[1024,1024]{1,0:T(8,128)(2,1)}) custom-call(bf16[8,128,1024]{2,1,0:T(8,128)(2,1)} %get-tuple-element.82.o_ref, bf16[8,128,1024]{2,1,0:T(8,128)(2,1)} %get-tuple-element.83.w_ref.refs_6_, bf16[1024,1024]{1,0:T(8,128)(2,1)} %x_ref.3, f32[1,1024]{1,0:T(1,128)} %bitcast.83), custom_call_target="tpu_custom_call" | custom-call | flops 7000000000 | bytes 14000000 | tf_op jit(solution)/shard_map/pallas_call | solution.py:174
  126.1 1.3 copy-done.19
  127.4 16.3 %shard_map.206 = (f32[1024,1024]{1,0:T(8,128)}, f32[1024,1024]{1,0:T(8,128)}) custom-call(s32[12]{0:T(128)} %pad_add_fusion.ids_ref, bf16[1024,1024]{1,0:T(8,128)(2,1)} %get-tuple-element.84.n_ref, bf16[1024,1024]{1,0:T(8,128)(2,1)} %multiply_convert_fusion.g_ref, bf16[8,128,1024]{2,1,0:T(8,128)(2,1)} %pad_maximum_fusion.1.refs_0_, ...), custom_call_target="tpu_custom_call" | custom-call | flops 14000000000 | bytes 28000000 | tf_op jit(solution)/shard_map/pallas_call | solution.py:269
  143.7 6.0 %all-gather.2.cloned.1.call-done = bf16[32,2,128,1024]{3,2,1,0:T(8,128)(2,1)} async-done(((bf16[1,2,128,1024]{3,2,1,0:T(8,128)(2,1)}), bf16[32,2,128,1024]{3,2,1,0:T(8,128)(2,1)}) %all-gather.2.cloned.1.call-update) | async-done | bytes 16777232 | tf_op jit(solution)/shard_map/all_gather | solution.py:530
  149.7 46.6 %shard_map.207 = (bf16[1024,1024]{1,0:T(8,128)(2,1)}, f32[1024,1024]{1,0:T(8,128)}, bf16[8,128,1024]{2,1,0:T(8,128)(2,1)}) custom-call(s32[12]{0:T(128)} %pad_add_fusion.ids_ref, bf16[1024,1024]{1,0:T(8,128)(2,1)} %get-tuple-element.84.n_ref, bf16[1024,1024]{1,0:T(8,128)(2,1)} %multiply_convert_fusion.g_ref, bf16[8,8,128,1024]{3,2,1,0:T(8,128)(2,1)} %bitcast.81, ...), custom_call_target="tpu_custom_call" | custom-call | flops 33999998976 | bytes 68000000 | tf_op jit(solution)/shard_map/pallas_call | solution.py:269
  196.2 34.2 %shard_map.208 = (bf16[8,384,1024]{2,1,0:T(8,128)(2,1)}, f32[8,1024]{1,0:T(8,128)}, f32[16,1024]{1,0:T(8,128)}) custom-call(s32[12]{0:T(128)} %pad_add_fusion.ids_ref, bf16[8,384,1024]{2,1,0:T(8,128)(2,1)} %get-tuple-element.90.qkv_ref, bf16[8,128,1024]{2,1,0:T(8,128)(2,1)} %get-tuple-element.82.o_ref, bf16[8,128,1024]{2,1,0:T(8,128)(2,1)} %get-tuple-element.91.do_ref, ...), custom_call_target="tpu_custom_call" | custom-call | flops 35000000512 | bytes 70000000 | tf_op jit(solution)/shard_map/pallas_call | solution.py:365
  230.8 1.2 collective-permute-done.13
  231.9 0.9 add.75
  232.8 0.5 collective-permute-start.14
  233.3 1.6 collective-permute-start.15
  234.9 2.4 collective-permute-start.16
  237.2 0.6 maximum_bitcast_fusion.2.dn_ref
  238.1 3.6 %collective-permute-done.15 = f32[16,1024]{1,0:T(8,128)S(1)} collective-permute-done((f32[16,1024]{1,0:T(8,128)S(1)}, f32[16,1024]{1,0:T(8,128)S(1)}, u32[]{:S(2)}, u32[]{:S(2)}) %collective-permute-start.15) | collective-permute-done | bytes 65568 | tf_op jit(solution)/shard_map/ppermute | solution.py:481
  241.7 1.3 collective-permute-start.17
  243.0 0.8 collective-permute-start.18
  243.8 1.5 collective-permute-start.19
  245.3 13.7 %shard_map.209 = bf16[1024,1024]{1,0:T(8,128)(2,1)} custom-call(bf16[8,384,1024]{2,1,0:T(8,128)(2,1)} %get-tuple-element.93.d_ref, bf16[8,384,1024]{2,1,0:T(8,128)(2,1)} %get-tuple-element.94.w_ref, f32[8,1024]{1,0:T(8,128)} %get-tuple-element.95.gl_ref, f32[8,1024]{1,0:T(8,128)} %maximum_bitcast_fusion.2.dn_ref, bf16[1024,1024]{1,0:T(8,128)(2,1)} %x_ref.3, ...), custom_call_target="tpu_custom_call" | custom-call | flops 12999999488 | bytes 26000000 | tf_op jit(solution)/shard_map/pallas_call | solution.py:405
  259.0 0.9 add_add_fusion
  259.9 0.6 fusion.34
  (110 shorter events, 3.8 us)
Async XLA Ops:
  7.2 2.0 copy-start.9
  7.2 142.5 %all-gather.2.cloned.1.call-start = ((), (), s32[]{:S(2)}) async-start(), calls=%async_computation | async-start | bytes 17301504 | tf_op jit(solution)/shard_map/all_gather | solution.py:530
  7.2 2.0 copy-start.8
  9.3 8.8 %copy-start.16 = (s32[1,4]{1,0:T(1,128)S(1)}, s32[1,4]{1,0:T(1,128)}, u32[]{:S(2)}) copy-start(s32[1,4]{1,0:T(1,128)} %param.28) | copy-start | bytes 52
  9.3 10.1 %copy-start.17 = (s32[1,20]{1,0:T(1,128)S(1)}, s32[1,20]{1,0:T(1,128)}, u32[]{:S(2)}) copy-start(s32[1,20]{1,0:T(1,128)} %param.29) | copy-start | bytes 244
  9.3 12.6 %copy-start.14 = (f32[4,1024]{1,0:T(4,128)S(1)}, f32[4,1024]{1,0:T(4,128)}, u32[]{:S(2)}) copy-start(f32[4,1024]{1,0:T(4,128)} %param.25) | copy-start | bytes 49156
  9.3 12.8 %copy-start.15 = (f32[4,1024]{1,0:T(4,128)S(1)}, f32[4,1024]{1,0:T(4,128)}, u32[]{:S(2)}) copy-start(f32[4,1024]{1,0:T(4,128)} %param.27) | copy-start | bytes 49156
  10.9 13.7 %copy-start.12 = (f32[1024,4]{0,1:T(4,128)S(1)}, f32[1024,4]{0,1:T(4,128)}, u32[]{:S(2)}) copy-start(f32[1024,4]{0,1:T(4,128)} %param.26) | copy-start | bytes 49156
  10.9 13.8 %copy-start.13 = (f32[1024,4]{0,1:T(4,128)S(1)}, f32[1024,4]{0,1:T(4,128)}, u32[]{:S(2)}) copy-start(f32[1024,4]{0,1:T(4,128)} %param.24) | copy-start | bytes 49156
  10.9 13.8 %copy-start.1 = (bf16[1024,1024]{1,0:T(8,128)(2,1)S(1)}, bf16[1024,1024]{1,0:T(8,128)(2,1)}, u32[]{:S(2)}) copy-start(bf16[1024,1024]{1,0:T(8,128)(2,1)} %x_ref.3) | copy-start | bytes 6291460
  10.9 61.8 %collective-permute-start.4 = (bf16[4,128,1024]{2,1,0:T(8,128)(2,1)}, bf16[4,128,1024]{2,1,0:T(8,128)(2,1)}, u32[]{:S(2)}, u32[]{:S(2)}) collective-permute-start(bf16[4,128,1024]{2,1,0:T(8,128)(2,1)} %get-tuple-element.101), channel_id=1, source_target_pairs={{0,1},{1,0},{2,3},{3,2},{4,5},{5,4},{6,7},{7,6},{8,9},{9,8},{10,11... | collective-permute-start | bytes 3145736 | tf_op jit(solution)/shard_map/ppermute | solution.py:481
  11.4 61.4 %collective-permute-start.2 = (bf16[4,128,1024]{2,1,0:T(8,128)(2,1)}, bf16[4,128,1024]{2,1,0:T(8,128)(2,1)S(1)}, u32[]{:S(2)}, u32[]{:S(2)}) collective-permute-start(bf16[4,128,1024]{2,1,0:T(8,128)(2,1)} %get-tuple-element.101), channel_id=1, source_target_pairs={{0,2},{1,3},{2,0},{3,1},{4,6},{5,7},{6,4},{7,5},{8,10},{9,11},{10,... | collective-permute-start | bytes 3145736 | tf_op jit(solution)/shard_map/ppermute | solution.py:481
  14.7 40.6 %collective-permute-start = (bf16[1,128,1024]{2,1,0:T(8,128)(2,1)}, bf16[1,128,1024]{2,1,0:T(8,128)(2,1)}, u32[]{:S(2)}, u32[]{:S(2)}) collective-permute-start(bf16[1,128,1024]{2,1,0:T(8,128)(2,1)} %fusion.6), channel_id=1, source_target_pairs={{0,4},{1,5},{2,6},{3,7},{4,0},{5,1},{6,2},{7,3},{8,12},{9,13},{10,... | collective-permute-start | bytes 786440 | tf_op jit(solution)/shard_map/ppermute | solution.py:481
  17.3 50.8 %collective-permute-start.1 = (bf16[1,128,1024]{2,1,0:T(8,128)(2,1)}, bf16[1,128,1024]{2,1,0:T(8,128)(2,1)}, u32[]{:S(2)}, u32[]{:S(2)}) collective-permute-start(bf16[1,128,1024]{2,1,0:T(8,128)(2,1)} %fusion.6), channel_id=1, source_target_pairs={{0,6},{1,7},{2,4},{3,5},{4,2},{5,3},{6,0},{7,1},{8,14},{9,15},{10,... | collective-permute-start | bytes 786440 | tf_op jit(solution)/shard_map/ppermute | solution.py:481
  24.7 1.6 copy-start.2
  24.7 1.6 copy-start.18
  27.0 2.6 copy-start
  27.0 2.1 copy-start.5
  27.0 2.3 copy-start.6
  29.6 1.5 copy-start.26
  36.9 6.8 %copy-start.7 = (bf16[1024,1024]{1,0:T(8,128)(2,1)S(1)}, bf16[1024,1024]{1,0:T(8,128)(2,1)}, u32[]{:S(2)}) copy-start(bf16[1024,1024]{1,0:T(8,128)(2,1)} %param.17) | copy-start | bytes 6291460
  69.2 25.8 %copy-start.10 = (bf16[2,128,1024]{2,1,0:T(8,128)(2,1)}, bf16[2,128,1024]{2,1,0:T(8,128)(2,1)S(1)}, u32[]{:S(2)}) copy-start(bf16[2,128,1024]{2,1,0:T(8,128)(2,1)S(1)} %pad_maximum_fusion.3.w0_ref) | copy-start | bytes 1572868
  69.2 25.1 %collective-permute-start.10 = (bf16[2,128,1024]{2,1,0:T(8,128)(2,1)S(1)}, bf16[2,128,1024]{2,1,0:T(8,128)(2,1)S(1)}, u32[]{:S(2)}, u32[]{:S(2)}) collective-permute-start(bf16[2,128,1024]{2,1,0:T(8,128)(2,1)S(1)} %pad_maximum_fusion.3.w0_ref), channel_id=1, source_target_pairs={{0,24},{8,16},{16,8},{24,0},{1,25},{9,17},{17,9},{25,1},{2,26},{10... | collective-permute-start | bytes 1572872 | tf_op jit(solution)/shard_map/ppermute | solution.py:481
  71.7 23.1 %collective-permute-start.6 = (bf16[2,128,1024]{2,1,0:T(8,128)(2,1)S(1)}, bf16[2,128,1024]{2,1,0:T(8,128)(2,1)S(1)}, u32[]{:S(2)}, u32[]{:S(2)}) collective-permute-start(bf16[2,128,1024]{2,1,0:T(8,128)(2,1)S(1)} %pad_maximum_fusion.3.w0_ref), channel_id=1, source_target_pairs={{0,8},{8,0},{16,24},{24,16},{1,9},{9,1},{17,25},{25,17},{2,10},{10... | collective-permute-start | bytes 1572872 | tf_op jit(solution)/shard_map/ppermute | solution.py:481
  72.3 22.1 %collective-permute-start.8 = (bf16[2,128,1024]{2,1,0:T(8,128)(2,1)S(1)}, bf16[2,128,1024]{2,1,0:T(8,128)(2,1)}, u32[]{:S(2)}, u32[]{:S(2)}) collective-permute-start(bf16[2,128,1024]{2,1,0:T(8,128)(2,1)S(1)} %pad_maximum_fusion.3.w0_ref), channel_id=1, source_target_pairs={{0,16},{8,24},{16,0},{24,8},{1,17},{9,25},{17,1},{25,9},{2,18},{10... | collective-permute-start | bytes 1572872 | tf_op jit(solution)/shard_map/ppermute | solution.py:481
  72.7 53.4 %collective-permute-start.12 = (bf16[4,2,128,1024]{3,2,1,0:T(8,128)(2,1)S(1)}, bf16[4,2,128,1024]{3,2,1,0:T(8,128)(2,1)S(1)}, u32[]{:S(2)}, u32[]{:S(2)}) collective-permute-start(bf16[4,2,128,1024]{3,2,1,0:T(8,128)(2,1)S(1)} %pad_maximum_fusion), channel_id=1, source_target_pairs={{0,1},{1,0},{2,3},{3,2},{4,5},{5,4},{6,7},{7,6},{8,9},{9,8},{10,11... | collective-permute-start | bytes 6291464 | tf_op jit(solution)/shard_map/ppermute | solution.py:481
  72.7 7.2 %copy-start.3 = (bf16[4,128,1024]{2,1,0:T(8,128)(2,1)}, bf16[4,128,1024]{2,1,0:T(8,128)(2,1)S(1)}, u32[]{:S(2)}) copy-start(bf16[4,128,1024]{2,1,0:T(8,128)(2,1)S(1)} %collective-permute-done.2) | copy-start | bytes 3145732
  72.7 13.8 %collective-permute-start.3 = (bf16[4,128,1024]{2,1,0:T(8,128)(2,1)S(1)}, bf16[4,128,1024]{2,1,0:T(8,128)(2,1)S(1)}, u32[]{:S(2)}, u32[]{:S(2)}) collective-permute-start(bf16[4,128,1024]{2,1,0:T(8,128)(2,1)S(1)} %collective-permute-done.2), channel_id=1, source_target_pairs={{0,1},{1,0},{2,3},{3,2},{4,5},{5,4},{6,7},{7,6},{8,9},{9,8},{10,11... | collective-permute-start | bytes 3145736 | tf_op jit(solution)/shard_map/ppermute | solution.py:481
  86.6 1.0 copy-start.4
  94.2 1.3 copy-start.21
  94.2 12.9 %collective-permute-start.11 = (bf16[2,128,1024]{2,1,0:T(8,128)(2,1)S(1)}, bf16[2,128,1024]{2,1,0:T(8,128)(2,1)S(1)}, u32[]{:S(2)}, u32[]{:S(2)}) collective-permute-start(bf16[2,128,1024]{2,1,0:T(8,128)(2,1)S(1)} %collective-permute-done.10.w3_ref), channel_id=1, source_target_pairs={{0,1},{1,0},{2,3},{3,2},{4,5},{5,4},{6,7},{7,6},{8,9},{9,8},{10,11... | collective-permute-start | bytes 1572872 | tf_op jit(solution)/shard_map/ppermute | solution.py:481
  94.4 12.8 %collective-permute-start.9 = (bf16[2,128,1024]{2,1,0:T(8,128)(2,1)}, bf16[2,128,1024]{2,1,0:T(8,128)(2,1)S(1)}, u32[]{:S(2)}, u32[]{:S(2)}) collective-permute-start(bf16[2,128,1024]{2,1,0:T(8,128)(2,1)} %collective-permute-done.8.w2_ref), channel_id=1, source_target_pairs={{0,1},{1,0},{2,3},{3,2},{4,5},{5,4},{6,7},{7,6},{8,9},{9,8},{10,11... | collective-permute-start | bytes 1572872 | tf_op jit(solution)/shard_map/ppermute | solution.py:481
  94.8 0.8 copy-start.20
  94.8 12.4 %collective-permute-start.7 = (bf16[2,128,1024]{2,1,0:T(8,128)(2,1)S(1)}, bf16[2,128,1024]{2,1,0:T(8,128)(2,1)S(1)}, u32[]{:S(2)}, u32[]{:S(2)}) collective-permute-start(bf16[2,128,1024]{2,1,0:T(8,128)(2,1)S(1)} %collective-permute-done.6.w1_ref), channel_id=1, source_target_pairs={{0,1},{1,0},{2,3},{3,2},{4,5},{5,4},{6,7},{7,6},{8,9},{9,8},{10,11... | collective-permute-start | bytes 1572872 | tf_op jit(solution)/shard_map/ppermute | solution.py:481
  94.9 12.3 %collective-permute-start.5 = (bf16[2,128,1024]{2,1,0:T(8,128)(2,1)S(1)}, bf16[2,128,1024]{2,1,0:T(8,128)(2,1)S(1)}, u32[]{:S(2)}, u32[]{:S(2)}) collective-permute-start(bf16[2,128,1024]{2,1,0:T(8,128)(2,1)S(1)} %pad_maximum_fusion.3.w0_ref), channel_id=1, source_target_pairs={{0,1},{1,0},{2,3},{3,2},{4,5},{5,4},{6,7},{7,6},{8,9},{9,8},{10,11... | collective-permute-start | bytes 1572872 | tf_op jit(solution)/shard_map/ppermute | solution.py:481
  107.2 0.8 copy-start.22
  107.2 0.9 copy-start.23
  107.2 1.1 copy-start.24
  107.2 1.2 copy-start.25
  126.1 1.3 copy-start.19
  230.4 1.5 collective-permute-start.13
  232.8 5.3 %collective-permute-start.14 = (f32[16,1024]{1,0:T(8,128)S(1)}, f32[16,1024]{1,0:T(8,128)S(1)}, u32[]{:S(2)}, u32[]{:S(2)}) collective-permute-start(f32[16,1024]{1,0:T(8,128)S(1)} %add.75), channel_id=1, source_target_pairs={{0,2},{1,3},{2,0},{3,1},{4,6},{5,7},{6,4},{7,5},{8,10},{9,11},{10,... | collective-permute-start | bytes 196616 | tf_op jit(solution)/shard_map/ppermute | solution.py:481
  233.3 8.4 %collective-permute-start.15 = (f32[16,1024]{1,0:T(8,128)S(1)}, f32[16,1024]{1,0:T(8,128)S(1)}, u32[]{:S(2)}, u32[]{:S(2)}) collective-permute-start(f32[16,1024]{1,0:T(8,128)S(1)} %add.75), channel_id=1, source_target_pairs={{0,4},{1,5},{2,6},{3,7},{4,0},{5,1},{6,2},{7,3},{8,12},{9,13},{10,... | collective-permute-start | bytes 196616 | tf_op jit(solution)/shard_map/ppermute | solution.py:481
  234.9 6.8 %collective-permute-start.16 = (f32[16,1024]{1,0:T(8,128)S(1)}, f32[16,1024]{1,0:T(8,128)S(1)}, u32[]{:S(2)}, u32[]{:S(2)}) collective-permute-start(f32[16,1024]{1,0:T(8,128)S(1)} %add.75), channel_id=1, source_target_pairs={{0,6},{1,7},{2,4},{3,5},{4,2},{5,3},{6,0},{7,1},{8,14},{9,15},{10,... | collective-permute-start | bytes 196616 | tf_op jit(solution)/shard_map/ppermute | solution.py:481
  241.7 3.6 %copy-start.11 = (f32[16,1024]{1,0:T(8,128)}, f32[16,1024]{1,0:T(8,128)S(1)}, u32[]{:S(2)}) copy-start(f32[16,1024]{1,0:T(8,128)S(1)} %add_add_fusion.1.event_ref) | copy-start | bytes 196612
  241.7 17.3 %collective-permute-start.17 = (f32[16,1024]{1,0:T(8,128)S(1)}, f32[16,1024]{1,0:T(8,128)S(1)}, u32[]{:S(2)}, u32[]{:S(2)}) collective-permute-start(f32[16,1024]{1,0:T(8,128)S(1)} %add_add_fusion.1.event_ref), channel_id=1, source_target_pairs={{0,8},{8,0},{16,24},{24,16},{1,9},{9,1},{17,25},{25,17},{2,10},{10... | collective-permute-start | bytes 196616 | tf_op jit(solution)/shard_map/ppermute | solution.py:481
  243.0 16.0 %collective-permute-start.18 = (f32[16,1024]{1,0:T(8,128)S(1)}, f32[16,1024]{1,0:T(8,128)S(1)}, u32[]{:S(2)}, u32[]{:S(2)}) collective-permute-start(f32[16,1024]{1,0:T(8,128)S(1)} %add_add_fusion.1.event_ref), channel_id=1, source_target_pairs={{0,16},{8,24},{16,0},{24,8},{1,17},{9,25},{17,1},{25,9},{2,18},{10... | collective-permute-start | bytes 196616 | tf_op jit(solution)/shard_map/ppermute | solution.py:481
  243.8 15.2 %collective-permute-start.19 = (f32[16,1024]{1,0:T(8,128)S(1)}, f32[16,1024]{1,0:T(8,128)S(1)}, u32[]{:S(2)}, u32[]{:S(2)}) collective-permute-start(f32[16,1024]{1,0:T(8,128)S(1)} %add_add_fusion.1.event_ref), channel_id=1, source_target_pairs={{0,24},{8,16},{16,8},{24,0},{1,25},{9,17},{17,9},{25,1},{2,26},{10... | collective-permute-start | bytes 196616 | tf_op jit(solution)/shard_map/ppermute | solution.py:481
Sparse Core Ops, SparseCore 0:
  10.9 138.7 all-gather.1
